TPU v7x, 32 devices: a whole 2x2x4 slice. The times are simulated.
32 devices in a mesh: grp: 2 (over y), gx: 4 (over z), gy: 2 (over x), gz: 2 (over core).
Axes of the slice: x: 2, y: 2, z: 4, core: 2. Of those that a mesh axis runs over, the one named last changes fastest.
Arguments:
- controls: float32 [40, 64, 512], P('gz', ('grp', 'gx'), 'gy'), parts along dimension 1, may hold values from -8.1 to 8.1
- anomalies: bfloat16 [2, 40, 64, 512], P(None, 'gz', ('grp', 'gx'), 'gy'), parts along dimension 2, may hold values from -6 to 6
- x_rates: float32 [64, 512], P(('grp', 'gx'), 'gy'), parts along dimension 0, may hold values from 0.3 to 1
- y_rates: float32 [64, 512], P(('grp', 'gx'), 'gy'), parts along dimension 0, may hold values from 0.3 to 1
- obs_cells: int32 [8, 2, 512], P(('grp', 'gx'), 'gy'), parts along dimension 0, may hold values from 0 to 2047
- obs_codes: int32 [8, 2, 512], P(('grp', 'gx'), 'gy'), parts along dimension 0, may hold values from 0 to 71
- obs_values: float32 [8, 2, 512], P(('grp', 'gx'), 'gy'), parts along dimension 0, may hold values from -6 to 6
- obs_weights: float32 [8, 2, 512], P(('grp', 'gx'), 'gy'), parts along dimension 0, may hold values from 0.25 to 4
- prev_gradient: float32 [40, 64, 512], P('gz', ('grp', 'gx'), 'gy'), parts along dimension 1, may hold values from -8.1 to 8.1
- prev_direction: float32 [40, 64, 512], P('gz', ('grp', 'gx'), 'gy'), parts along dimension 1, may hold values from -6 to 6
Outputs:
- gradient: float32 [40, 64, 512], P('gz', ('grp', 'gx'), 'gy'), parts along dimension 1
- direction: float32 [40, 64, 512], P('gz', ('grp', 'gx'), 'gy'), parts along dimension 1
- increment: float32 [2, 64, 512], P(None, ('grp', 'gx'), 'gy'), parts along dimension 1
There are 2 independent parts, one for each index of `grp`. A program takes and returns all parts, laid end to end along the dimension named above; each array names one. Nothing has to cross between parts.
Inputs may be any that keep to these rules, and one draw needn't show every extreme that they name: obs_cells holds x * 256 + y for the cell (x, y) of the tile.
All inputs are finite; a program needn't handle non-finite values.
Results may differ from a plain program's by a relative error of at most 0.0003.
Values sent between devices are 32-bit elements; how exact they have to be, the bound alone decides.
A program may use at most 128 MiB of HBM per device.

v0:
```python
import math

import jax
import jax.numpy as jnp
from jax import lax
from jax.sharding import PartitionSpec as P

K = 40
NDIR = 72


def prefix(part, axis, combine, identity, reverse):
    count = lax.axis_size(axis)
    place = lax.axis_index(axis)
    ahead = count - 1 - place if reverse else place
    gathered = jax.tree.map(lambda a: lax.all_gather(a, axis), part)
    state = jax.tree.map(lambda a, e: jnp.zeros_like(a) + jnp.asarray(e, a.dtype), part, identity)

    def one(turn, state):
        source = count - 1 - turn if reverse else turn
        return combine(
            state, jax.tree.map(lambda a: lax.dynamic_index_in_dim(a, source, 0, False), gathered)
        )

    return lax.fori_loop(0, ahead, one, state)


def compose(earlier, latter):
    first_mult, first_add = earlier
    second_mult, second_add = latter
    return (first_mult * second_mult, second_mult * first_add + second_add)


def local_run(factor_field, weights, along_dim, reverse):
    spread_field = jnp.broadcast_to(factor_field, weights.shape)
    return lax.associative_scan(compose, (spread_field, weights), reverse=reverse, axis=along_dim)


def chain_states(factor_field, weights, along_dim, reverse):
    products, states = local_run(factor_field, weights, along_dim, reverse)
    boundary = 0 if reverse else weights.shape[along_dim] - 1
    total_mult = lax.index_in_dim(products[0:1], boundary, along_dim, keepdims=False)
    total_add = lax.index_in_dim(states, boundary, along_dim, keepdims=False)
    neutral = (jnp.ones_like(total_mult), jnp.zeros_like(total_add))
    if along_dim == 1:
        _, incoming = prefix((total_mult, total_add), "gx", compose, neutral, reverse)
    else:
        _, incoming = prefix((total_mult, total_add), "gy", compose, neutral, reverse)
    return states + products * jnp.expand_dims(incoming, along_dim)


def smooth(factor_field, gain_field, values, along_dim, adjoint, runner):
    leading = factor_field * values if adjoint else gain_field * values
    inward = runner(factor_field, leading, along_dim, False)
    outward = runner(factor_field, gain_field * inward, along_dim, True)
    return gain_field / factor_field * outward if adjoint else outward


def shards(
    controls,
    anomalies,
    x_rates,
    y_rates,
    obs_cells,
    obs_codes,
    obs_values,
    obs_weights,
    prev_gradient,
    prev_direction,
):
    x_factor = x_rates[None]
    y_factor = y_rates[None]
    x_scales = jnp.sqrt(1.0 - x_factor * x_factor)
    y_scales = jnp.sqrt(1.0 - y_factor * y_factor)
    spread = 1.0 / math.sqrt(K - 1)

    def pass_first(values, adjoint):
        return smooth(x_factor, x_scales, values, 1, adjoint, chain_states)

    def pass_second(values, adjoint):
        return smooth(y_factor, y_scales, values, 2, adjoint, chain_states)

    filtered = pass_second(pass_first(controls, False), False)
    partial_value = jnp.sum(anomalies.astype(jnp.float32) * filtered[None], axis=1) * spread
    increment = lax.psum(partial_value, "gz")
    located = obs_cells.reshape(-1)
    bearing = obs_codes.reshape(-1).astype(jnp.float32) * (2.0 * math.pi / NDIR)
    cosine = jnp.cos(bearing)
    sines = jnp.sin(bearing)
    flat_east = increment[0].reshape(-1)
    flat_north = increment[1].reshape(-1)
    projected = cosine * flat_east[located] + sines * flat_north[located]
    misfit = obs_weights.reshape(-1) * (projected - obs_values.reshape(-1))
    cell_count = flat_east.shape[0]
    back_east = (
        jnp.zeros((cell_count,), jnp.float32)
        .at[located]
        .add(cosine * misfit)
        .reshape(increment.shape[1:])
    )
    back_north = (
        jnp.zeros((cell_count,), jnp.float32)
        .at[located]
        .add(sines * misfit)
        .reshape(increment.shape[1:])
    )
    pulled = (
        anomalies[0].astype(jnp.float32) * back_east[None]
        + anomalies[1].astype(jnp.float32) * back_north[None]
    ) * spread
    gradient = controls + pass_first(pass_second(pulled, True), True)
    numerator, denominator = lax.psum(
        (jnp.sum(gradient * (gradient - prev_gradient)), jnp.sum(prev_gradient * prev_gradient)),
        ("gx", "gy", "gz"),
    )
    direction = -gradient + numerator / denominator * prev_direction
    return (gradient, direction, increment)


def solution(mesh):
    in_specs = (
        P("gz", ("grp", "gx"), "gy"),
        P(None, "gz", ("grp", "gx"), "gy"),
        P(("grp", "gx"), "gy"),
        P(("grp", "gx"), "gy"),
        P(("grp", "gx"), "gy", None),
        P(("grp", "gx"), "gy", None),
        P(("grp", "gx"), "gy", None),
        P(("grp", "gx"), "gy", None),
        P("gz", ("grp", "gx"), "gy"),
        P("gz", ("grp", "gx"), "gy"),
    )
    out_specs = (
        P("gz", ("grp", "gx"), "gy"),
        P("gz", ("grp", "gx"), "gy"),
        P(None, ("grp", "gx"), "gy"),
    )
    return jax.shard_map(shards, mesh=mesh, in_specs=in_specs, out_specs=out_specs, check_vma=False)
```

profile of v0, /device:TPU:0, one launch (start us, length us, event | category | flops | bytes accessed | tf_op | source)
XLA Modules:
  0.0 457.3 jit_solution(16847866725613544336)
XLA Ops:
  5.6 14.9 %all-gather = f32[80,1,256]{2,1,0:T(1,128)S(1)} all-gather(f32[20,1,256]{2,1,0:T(1,128)S(1)} %slice_add_fusion.21), channel_id=2, replica_groups=mesh['grp'=2,'gx'=4,'gy'=2,'gz'=2] {'gx'}, dimensions={0}, use_global_device_ids=true | all-gather | bytes 102400 | tf_op jit(solution)/shard_map/all_gather | solution.py:16
  21.2 11.1 %all_gather.40 = f32[4,1,256]{2,1,0:T(1,128)S(1)} all-gather(f32[1,1,256]{2,1,0:T(1,128)S(1)} %slice_add_fusion.27), channel_id=1, replica_groups=mesh['grp'=2,'gx'=4,'gy'=2,'gz'=2] {'gx'}, dimensions={0}, use_global_device_ids=true | all-gather | bytes 5120 | tf_op jit(solution)/shard_map/all_gather | solution.py:16
  36.5 13.2 %all-gather.1 = f32[80,1,256]{2,1,0:T(1,128)S(1)} all-gather(f32[20,1,256]{2,1,0:T(1,128)S(1)} %slice_add_fusion.18), channel_id=3, replica_groups=mesh['grp'=2,'gx'=4,'gy'=2,'gz'=2] {'gx'}, dimensions={0}, use_global_device_ids=true | all-gather | bytes 102400 | tf_op jit(solution)/shard_map/all_gather | solution.py:16
  50.3 7.6 %all_gather.42 = f32[4,1,256]{2,1,0:T(1,128)S(1)} all-gather(f32[1,1,256]{2,1,0:T(1,128)S(1)} %slice_add_fusion.26), channel_id=1, replica_groups=mesh['grp'=2,'gx'=4,'gy'=2,'gz'=2] {'gx'}, dimensions={0}, use_global_device_ids=true | all-gather | bytes 5120 | tf_op jit(solution)/shard_map/all_gather | solution.py:16
  99.1 14.4 %pad.503 = f32[20,8,32]{2,1,0:T(8,128)S(1)} pad(f32[20,8,16]{2,1,0:T(8,128)S(1)} %add.982, f32[]{:T(128)} %constant.182.clone.1), padding=0_0_0x0_0_0x1_0_1 | pad | bytes 30724 | tf_op jit(solution)/shard_map/pad | solution.py:36
  130.0 4.0 pad.493
  142.9 4.0 pad.492
  147.3 4.4 all-gather.3
  151.8 4.0 pad.509
  156.2 4.0 pad.508
  160.4 4.2 all-gather.2
  229.2 4.0 pad.525
  242.2 4.0 pad.524
  246.5 4.4 all-gather.5
  251.1 4.0 pad.541
  255.3 4.0 pad.540
  259.5 4.2 all-gather.4
  320.9 4.0 pad.557
  327.9 4.0 pad.556
  332.2 4.4 all-gather.6
  386.7 4.4 all-gather.7
  393.7 13.2 %all-gather.8 = f32[80,1,256]{2,1,0:T(1,128)S(1)} all-gather(f32[20,1,256]{2,1,0:T(1,128)S(1)} %slice_add_fusion.15), channel_id=10, replica_groups=mesh['grp'=2,'gx'=4,'gy'=2,'gz'=2] {'gx'}, dimensions={0}, use_global_device_ids=true | all-gather | bytes 102400 | tf_op jit(solution)/shard_map/all_gather | solution.py:16
  409.6 13.2 %all-gather.9 = f32[80,1,256]{2,1,0:T(1,128)S(1)} all-gather(f32[20,1,256]{2,1,0:T(1,128)S(1)} %slice_add_fusion.12), channel_id=11, replica_groups=mesh['grp'=2,'gx'=4,'gy'=2,'gz'=2] {'gx'}, dimensions={0}, use_global_device_ids=true | all-gather | bytes 102400 | tf_op jit(solution)/shard_map/all_gather | solution.py:16
  425.0 30.1 %all-reduce.132 = (f32[]{:T(128)}, f32[]{:T(128)}) all-reduce(f32[]{:T(128)} %get-tuple-element.604, f32[]{:T(128)} %get-tuple-element.603), channel_id=1, replica_groups=mesh['grp'=2,'gx'=4,'gy'=2,'gz'=2] {'gx','gy','gz'}, use_global_device_ids=true, to_apply=%region_21.22 | all-reduce | flops 2 | bytes 16 | tf_op jit(solution)/shard_map/psum | solution.py:112
  (639 shorter events, 268.1 us)
Async XLA Ops:
  2.4 0.7 copy-start.5
  58.6 0.7 copy-start.6
  264.6 0.9 copy-start
  264.6 4.9 %copy-start.9 = (s32[1,1,512]{2,1,0:T(1,128)S(1)}, s32[1,1,512]{2,1,0:T(1,128)}, u32[]{:S(2)}) copy-start(s32[1,1,512]{2,1,0:T(1,128)} %param.30) | copy-start | bytes 6148
  268.9 0.6 copy-start.7
  272.7 3.2 copy-start.8
  276.0 0.7 copy-start.11
  276.0 0.7 copy-start.10
  423.3 0.9 copy-start.1
  423.3 1.0 copy-start.4
  424.3 32.1 %copy-start.3 = (f32[20,8,256]{2,1,0:T(8,128)S(1)}, f32[20,8,256]{2,1,0:T(8,128)}, u32[]{:S(2)}) copy-start(f32[20,8,256]{2,1,0:T(8,128)} %param.35) | copy-start | bytes 491524
  425.0 32.1 %copy-start.2 = (f32[20,8,256]{2,1,0:T(8,128)}, f32[20,8,256]{2,1,0:T(8,128)S(1)}, u32[]{:S(2)}) copy-start(f32[20,8,256]{2,1,0:T(8,128)S(1)} %get-tuple-element.694) | copy-start | bytes 491524
where the time goes:
time: 455 us; the launch traced here: 457 us
  local copies, waits for them, and re-layouts  297 us (65%)
  blocking collectives  133 us (29%)
  other arithmetic  21.2 us (5%)
  between operations  5.37 us (1%)
    pad x108, local copies, waits for them, and re-layouts, local_run(): lax.associative_scan(compose, (spread_field, weights), reverse=reverse, a...  196 us
    all_gather x12, blocking collectives, prefix(): gathered = jax.tree.map(lambda a: lax.all_gather(a, axis), part)  99.1 us
    slice x181, local copies, waits for them, and re-layouts, local_run(): lax.associative_scan(compose, (spread_field, weights), reverse=reverse, a...  86.7 us
    psum x1, blocking collectives, shards(): lax.psum((jnp.sum(gradient * (gradient - prev_gradient)), jnp.sum(prev_gr...  30.1 us

commit v1 on v0

v1 whole, which is shorter than its diff:
```python
import functools
import math

import jax
import jax.numpy as jnp
from jax import lax
from jax.experimental import pallas as pl
from jax.experimental.pallas import tpu as pltpu
from jax.sharding import PartitionSpec as P

NDIR = 72
LANES = 128
ROWS = 8
MESH = pl.DeviceIdType.MESH


def rolled(values, shift, axis):
    return pltpu.roll(values, shift % values.shape[axis], axis)


def ladder(rates, axis, reverse):
    size = rates.shape[axis]
    place = lax.broadcasted_iota(jnp.int32, rates.shape, axis)
    factor = jnp.where(place == (size - 1 if reverse else 0), 0.0, rates)
    steps = []
    d = 1
    while d < size:
        shift = -d if reverse else d
        steps.append((shift, factor))
        factor = factor * rolled(factor, shift, axis)
        d *= 2
    return steps


def run(steps, values, axis):
    for shift, factor in steps:
        values = values + factor * rolled(values, shift, axis)
    return values


class Line:
    def __init__(self, rates, axis):
        self.axis = axis
        self.rates = rates
        self.scales = jnp.sqrt(1.0 - rates * rates)
        self.forward = ladder(rates, axis, False)
        self.backward = ladder(rates, axis, True)
        place = lax.broadcasted_iota(jnp.int32, rates.shape, axis)
        self.onward = run(self.forward, jnp.where(place == 0, rates, 0.0), axis)
        self.back = run(self.backward, jnp.where(place == rates.shape[axis] - 1, rates, 0.0), axis)
        self.echo = run(self.backward, self.scales * self.onward, axis)

    def local(self, leading):
        inward = run(self.forward, leading, self.axis)
        return inward, run(self.backward, self.scales * inward, self.axis)


def split_three(values):
    high = values.astype(jnp.bfloat16)
    rest = values - high.astype(jnp.float32)
    middle = rest.astype(jnp.bfloat16)
    low = (rest - middle.astype(jnp.float32)).astype(jnp.bfloat16)
    return jnp.concatenate([high, middle, low], axis=0)


def kernel(
    sizes,
    controls_h, anomalies_h, x_rates_h, y_rates_h, cells_h, codes_h, values_h, weights_h, prev_h,
    gradient_h, increment_h, ratio_ref,
    controls, anomalies, x_rates, y_rates, cells, codes, values, weights, prev,
    gradient, increment, work, enter, slots_x, slots_y, slots_z, slots_s,
    load_sem, store_sem, send_x, recv_x, send_y, recv_y, send_z, recv_z, send_s, recv_s,
):
    n_gx, n_gy, n_gz = sizes
    total = n_gx * n_gy * n_gz
    gx, gy, gz = (lax.axis_index(name) for name in ("gx", "gy", "gz"))
    me = (gx * n_gy + gy) * n_gz + gz
    members, rows, columns = controls.shape
    parts = [slice(at, at + LANES) for at in range(0, columns, LANES)]
    spread = 1.0 / math.sqrt(members * n_gz - 1)

    def place_of(peer):
        return {"gx": peer // (n_gy * n_gz), "gy": peer // n_gz % n_gy, "gz": peer % n_gz}

    def each_peer(body):
        if total <= 32:
            for off in range(1, total):
                body(lax.rem(me + off, total))
        else:
            lax.fori_loop(1, total, lambda off, c: (body(lax.rem(me + off, total)), c)[1], 0)

    barrier = pltpu.get_barrier_semaphore()
    each_peer(lambda peer: pl.semaphore_signal(
        barrier, inc=1, device_id=place_of(peer), device_id_type=MESH))

    loads = [
        pltpu.make_async_copy(src, dst, load_sem.at[i])
        for i, (src, dst) in enumerate((
            (x_rates_h, x_rates), (controls_h, controls), (y_rates_h, y_rates),
            (anomalies_h, anomalies), (cells_h, cells), (codes_h, codes), (values_h, values),
            (weights_h, weights), (prev_h, prev)))
    ]
    for load in loads:
        load.start()

    row_at = lax.broadcasted_iota(jnp.int32, (rows, LANES), 0)
    lane_at = lax.broadcasted_iota(jnp.int32, (rows, LANES), 1)

    def pack_rows(blocks, from_row, group):
        tile = jnp.zeros((rows, LANES), jnp.float32)
        for s, block in enumerate(blocks[group * rows:(group + 1) * rows]):
            tile = jnp.where(row_at == s, rolled(block, s - from_row, 0), tile)
        return tile

    def local_x(leading, lines, turn):
        outs = []
        for part, line, lead in zip(parts, lines, leading):
            inward, outward = line.local(lead)
            ends = [inward[k] for k in range(members)] + [line.onward[0]]
            heads = [outward[k] for k in range(members)] + [line.echo[0]]
            for group in range(slots_x.shape[3] // rows):
                here = pl.ds(group * rows, rows)
                slots_x[turn, gx, 0, here, part] = pack_rows(ends, rows - 1, group)
                slots_x[turn, gx, 1, here, part] = pack_rows(heads, 0, group)
            outs.append(outward)
        return outs

    def copy_x(turn, kind, source, peer):
        return pltpu.make_async_remote_copy(
            src_ref=slots_x.at[turn, source, kind], dst_ref=slots_x.at[turn, source, kind],
            send_sem=send_x.at[turn, kind, peer], recv_sem=recv_x.at[turn, kind, source],
            device_id={"gx": peer}, device_id_type=MESH)

    def start_x(turn):
        for off in range(1, n_gx):
            peer = lax.rem(gx + off, n_gx)
            copy_x(turn, 0, gx, peer).start()

            @pl.when(peer < gx)
            def _():
                copy_x(turn, 1, gx, peer).start()

    def finish_x(turn, lines, outs):
        for off in range(1, n_gx):
            source = lax.rem(gx + off, n_gx)
            copy_x(turn, 0, source, source).wait_recv()

            @pl.when(source > gx)
            def _():
                copy_x(turn, 1, source, source).wait_recv()

        results = []
        for part, line, outward in zip(parts, lines, outs):
            ends = [slots_x[turn, t, 0, :, part] for t in range(n_gx)]
            heads = [slots_x[turn, t, 1, :, part] for t in range(n_gx)]
            through = [v[members:members + 1] for v in ends]
            echoes = [v[members:members + 1] for v in heads]
            state = jnp.zeros_like(ends[0])
            states = [state]
            mine = state
            for t in range(n_gx - 1):
                state = through[t] * state + ends[t]
                states.append(state)
                mine = jnp.where(gx == t + 1, state, mine)
            enter[0, :, part] = mine
            state = jnp.zeros_like(ends[0])
            mine = state
            for t in range(n_gx - 1, 0, -1):
                state = through[t] * state + heads[t] + echoes[t] * states[t]
                mine = jnp.where(gx == t - 1, state, mine)
            enter[1, :, part] = mine
            for k in range(members):
                first = jnp.broadcast_to(enter[0, k:k + 1, part], (rows, LANES))
                second = jnp.broadcast_to(enter[1, k:k + 1, part], (rows, LANES))
                work[k, :, part] = outward[k] + line.echo[0] * first + line.back[0] * second
            results.append(work[:, :, part])
        return results

    def pack_lanes(field, from_lane):
        tile = jnp.zeros((rows, LANES), jnp.float32)
        for k in range(members):
            tile = jnp.where(lane_at == k, rolled(field[k], k - from_lane, 1), tile)
        return tile

    def across(tile, lane):
        return jnp.broadcast_to(tile[:, lane:lane + 1], (rows, LANES))

    def local_y(leading, lines, factors, turn):
        outs, ends, heads = [], [], []
        for line, lead in zip(lines, leading):
            inward, outward = line.local(lead)
            ends.append(pack_lanes(inward, LANES - 1))
            heads.append(pack_lanes(outward, 0))
            outs.append(outward)
        through, echoes, whole_through, whole_echo = factors
        state = jnp.zeros((rows, LANES), jnp.float32)
        states = []
        for a, f in zip(through, ends):
            states.append(state)
            state = a * state + f
        back = jnp.zeros((rows, LANES), jnp.float32)
        for a, c, b, h in reversed(list(zip(through, echoes, heads, states))):
            back = a * back + b + c * h
        slots_y[turn, gy, 0] = jnp.where(lane_at == members, whole_through, state)
        slots_y[turn, gy, 1] = jnp.where(lane_at == members, whole_echo, back)
        return outs, ends, heads

    def copy_y(turn, source, peer):
        return pltpu.make_async_remote_copy(
            src_ref=slots_y.at[turn, source], dst_ref=slots_y.at[turn, source],
            send_sem=send_y.at[turn, peer], recv_sem=recv_y.at[turn, source],
            device_id={"gy": peer}, device_id_type=MESH)

    def start_y(turn):
        for off in range(1, n_gy):
            copy_y(turn, gy, lax.rem(gy + off, n_gy)).start()

    def finish_y(turn, lines, factors, held):
        outs, ends, heads = held
        through, echoes, _, _ = factors
        for off in range(1, n_gy):
            source = lax.rem(gy + off, n_gy)
            copy_y(turn, source, source).wait_recv()
        state = jnp.zeros((rows, LANES), jnp.float32)
        states = [state]
        first = state
        for t in range(n_gy - 1):
            tile = slots_y[turn, t, 0]
            state = across(tile, members) * state + tile
            states.append(state)
            first = jnp.where(gy == t + 1, state, first)
        state = jnp.zeros((rows, LANES), jnp.float32)
        second = state
        for t in range(n_gy - 1, 0, -1):
            tile = slots_y[turn, t, 1]
            state = across(slots_y[turn, t, 0], members) * state + tile + across(tile, members) * states[t]
            second = jnp.where(gy == t - 1, state, second)
        firsts, seconds = [], []
        for a, f in zip(through, ends):
            firsts.append(first)
            first = a * first + f
        for a, c, b, h in reversed(list(zip(through, echoes, heads, firsts))):
            seconds.insert(0, second)
            second = a * second + b + c * h
        return [
            [outward[k] + line.echo[0] * across(h, k) + line.back[0] * across(b, k) for k in range(members)]
            for line, outward, h, b in zip(lines, outs, firsts, seconds)
        ]

    loads[0].wait()
    lines_x = [Line(x_rates[:, part][None], 1) for part in parts]
    loads[1].wait()
    held = local_x([line.scales * controls[:, :, part] for part, line in zip(parts, lines_x)], lines_x, 0)
    pl.semaphore_wait(barrier, total - 1)
    start_x(0)

    loads[2].wait()
    lines_y = [Line(y_rates[:, part][None], 2) for part in parts]
    through_y = [across(line.onward[0], LANES - 1) for line in lines_y]
    echoes_y = [across(line.echo[0], 0) for line in lines_y]
    whole_through = jnp.ones((rows, LANES), jnp.float32)
    reach = []
    for a in through_y:
        reach.append(whole_through)
        whole_through = whole_through * a
    whole_echo = jnp.zeros((rows, LANES), jnp.float32)
    for a, c, h in reversed(list(zip(through_y, echoes_y, reach))):
        whole_echo = a * whole_echo + c * h
    factors_y = (through_y, echoes_y, whole_through, whole_echo)

    for load in loads[3:]:
        load.wait()
    n_obs = cells.shape[-1]
    cell = cells[0]
    bits = columns.bit_length() - 1
    cell_row = lax.shift_right_logical(cell, jnp.full_like(cell, bits))
    cell_column = cell & (columns - 1)
    bearing = codes[0].astype(jnp.float32) * (2.0 * math.pi / NDIR)
    cosine = jnp.cos(bearing)
    sine = jnp.sin(bearing)
    at_column = (lax.broadcasted_iota(jnp.int32, (columns, n_obs), 0) == cell_column).astype(
        jnp.float32).astype(jnp.bfloat16)
    in_row = lax.broadcasted_iota(jnp.int32, (rows, n_obs), 0) == cell_row
    toward = jnp.concatenate([jnp.where(in_row, cosine, 0.0), jnp.where(in_row, sine, 0.0)], axis=0)
    before = prev[...]
    denominator = jnp.sum(jnp.sum(before * before, axis=0), axis=0, keepdims=True)

    filtered = finish_x(0, lines_x, held)

    held = local_y([line.scales * v for line, v in zip(lines_y, filtered)], lines_y, factors_y, 0)
    start_y(0)
    filtered = finish_y(0, lines_y, factors_y, held)

    for c in range(2):
        for part, field in zip(parts, filtered):
            summed = jnp.zeros((rows, LANES), jnp.float32)
            for k in range(members):
                summed = summed + anomalies[c, k, :, part].astype(jnp.float32) * field[k]
            slots_z[gz, c, :, part] = summed

    def copy_z(source, peer):
        return pltpu.make_async_remote_copy(
            src_ref=slots_z.at[source], dst_ref=slots_z.at[source],
            send_sem=send_z.at[peer], recv_sem=recv_z.at[source],
            device_id={"gz": peer}, device_id_type=MESH)

    for off in range(1, n_gz):
        copy_z(gz, lax.rem(gz + off, n_gz)).start()
    for off in range(1, n_gz):
        source = lax.rem(gz + off, n_gz)
        copy_z(source, source).wait_recv()
    grown = slots_z[0]
    for t in range(1, n_gz):
        grown = grown + slots_z[t]
    grown = grown * spread
    increment[...] = grown
    store_increment = pltpu.make_async_copy(increment, increment_h, store_sem.at[0])
    store_increment.start()

    lifted = jnp.dot(
        split_three(jnp.concatenate([grown[0], grown[1]], axis=0)), at_column,
        preferred_element_type=jnp.float32)
    lifted = lifted[:2 * rows] + (lifted[2 * rows:4 * rows] + lifted[4 * rows:])
    projected = jnp.sum(lifted * toward, axis=0, keepdims=True)
    misfit = weights[0] * (projected - values[0])
    back = lax.dot_general(
        split_three(toward * misfit), at_column, (((1,), (1,)), ((), ())),
        preferred_element_type=jnp.float32)
    back = (back[:2 * rows] + (back[2 * rows:4 * rows] + back[4 * rows:])) * spread

    leading = []
    for part, line in zip(parts, lines_y):
        pulled = (anomalies[0, :, :, part].astype(jnp.float32) * back[None, :rows, part]
                  + anomalies[1, :, :, part].astype(jnp.float32) * back[None, rows:, part])
        leading.append(line.rates * pulled)
    held = local_y(leading, lines_y, factors_y, 1)
    start_y(1)
    smoothed = finish_y(1, lines_y, factors_y, held)
    leading = []
    for part, line_x, line_y, field in zip(parts, lines_x, lines_y, smoothed):
        scale = (line_y.scales / line_y.rates * line_x.rates)[0]
        for k in range(members):
            work[k, :, part] = scale * field[k]
        leading.append(work[:, :, part])
    held = local_x(leading, lines_x, 1)
    start_x(1)
    smoothed = finish_x(1, lines_x, held)
    numerator = jnp.zeros((rows, LANES), jnp.float32)
    for part, line, field in zip(parts, lines_x, smoothed):
        new = controls[:, :, part] + line.scales / line.rates * field
        gradient[:, :, part] = new
        numerator = numerator + jnp.sum(new * (new - prev[:, :, part]), axis=0)
    store_gradient = pltpu.make_async_copy(gradient, gradient_h, store_sem.at[1])
    store_gradient.start()

    halves = denominator[:, parts[0]]
    for part in parts[1:]:
        halves = halves + denominator[:, part]
    slots_s[me, 0:1] = jnp.sum(numerator, axis=0, keepdims=True)
    slots_s[me, 1:2] = halves

    def copy_s(source, peer):
        return pltpu.make_async_remote_copy(
            src_ref=slots_s.at[source], dst_ref=slots_s.at[source],
            send_sem=send_s.at[peer], recv_sem=recv_s.at[source],
            device_id=place_of(peer), device_id_type=MESH)

    each_peer(lambda peer: copy_s(me, peer).start())
    each_peer(lambda peer: copy_s(peer, peer).wait_recv())
    sums = jnp.sum(jnp.sum(slots_s[...], axis=0), axis=1, keepdims=True)
    ratio_ref[...] = jnp.broadcast_to(sums[0:1] / sums[1:2], ratio_ref.shape)

    each_peer(lambda peer: copy_s(me, peer).wait_send())
    for turn in range(2):
        for off in range(1, n_gx):
            peer = lax.rem(gx + off, n_gx)
            copy_x(turn, 0, gx, peer).wait_send()

            @pl.when(peer < gx)
            def _():
                copy_x(turn, 1, gx, peer).wait_send()

        for off in range(1, n_gy):
            copy_y(turn, gy, lax.rem(gy + off, n_gy)).wait_send()
    for off in range(1, n_gz):
        copy_z(gz, lax.rem(gz + off, n_gz)).wait_send()
    store_increment.wait()
    store_gradient.wait()


def shards(
    controls,
    anomalies,
    x_rates,
    y_rates,
    obs_cells,
    obs_codes,
    obs_values,
    obs_weights,
    prev_gradient,
    prev_direction,
):
    n_gx, n_gy, n_gz = (lax.axis_size(name) for name in ("gx", "gy", "gz"))
    total = n_gx * n_gy * n_gz
    members, rows, columns = controls.shape
    packed = -(-(members + 1) // rows) * rows
    args = (controls, anomalies, x_rates, y_rates, obs_cells, obs_codes, obs_values, obs_weights, prev_gradient)
    dma = pltpu.SemaphoreType.DMA
    gradient, increment, ratio = pl.pallas_call(
        functools.partial(kernel, (n_gx, n_gy, n_gz)),
        out_shape=(
            jax.ShapeDtypeStruct(controls.shape, jnp.float32),
            jax.ShapeDtypeStruct((2, rows, columns), jnp.float32),
            jax.ShapeDtypeStruct((ROWS, LANES), jnp.float32),
        ),
        in_specs=[pl.BlockSpec(memory_space=pl.ANY)] * len(args),
        out_specs=(
            pl.BlockSpec(memory_space=pl.ANY),
            pl.BlockSpec(memory_space=pl.ANY),
            pl.BlockSpec(memory_space=pltpu.VMEM),
        ),
        scratch_shapes=[pltpu.VMEM(a.shape, a.dtype) for a in args] + [
            pltpu.VMEM(controls.shape, jnp.float32),
            pltpu.VMEM((2, rows, columns), jnp.float32),
            pltpu.VMEM(controls.shape, jnp.float32),
            pltpu.VMEM((2, packed, columns), jnp.float32),
            pltpu.VMEM((2, n_gx, 2, packed, columns), jnp.float32),
            pltpu.VMEM((2, n_gy, 2, rows, LANES), jnp.float32),
            pltpu.VMEM((n_gz, 2, rows, columns), jnp.float32),
            pltpu.VMEM((total, 2, LANES), jnp.float32),
            dma((len(args),)), dma((2,)),
            dma((2, 2, n_gx)), dma((2, 2, n_gx)),
            dma((2, n_gy)), dma((2, n_gy)),
            dma((n_gz,)), dma((n_gz,)),
            dma((total,)), dma((total,)),
        ],
        compiler_params=pltpu.CompilerParams(
            collective_id=0, has_side_effects=True, vmem_limit_bytes=40 * 1024 * 1024
        ),
    )(*args)
    direction = ratio[0, 0] * prev_direction - gradient
    return (gradient, direction, increment)


def solution(mesh):
    in_specs = (
        P("gz", ("grp", "gx"), "gy"),
        P(None, "gz", ("grp", "gx"), "gy"),
        P(("grp", "gx"), "gy"),
        P(("grp", "gx"), "gy"),
        P(("grp", "gx"), "gy", None),
        P(("grp", "gx"), "gy", None),
        P(("grp", "gx"), "gy", None),
        P(("grp", "gx"), "gy", None),
        P("gz", ("grp", "gx"), "gy"),
        P("gz", ("grp", "gx"), "gy"),
    )
    out_specs = (
        P("gz", ("grp", "gx"), "gy"),
        P("gz", ("grp", "gx"), "gy"),
        P(None, ("grp", "gx"), "gy"),
    )
    return jax.shard_map(shards, mesh=mesh, in_specs=in_specs, out_specs=out_specs, check_vma=False)
```

time: 455 us -> 40.5 us (0.09)
  local copies, waits for them, and re-layouts: 297 us -> 8.64 us
  blocking collectives: 133 us -> 0 us
  Pallas kernels: 0 us -> 29.5 us
  other arithmetic: 21.2 us -> 1.34 us
  between operations: 5.37 us -> 0.66 us
    pad x108 -> x0, local copies, waits for them, and re-layouts: 196 us -> none  [local_run(): lax.associative_scan(compose, (spread_field, weights), reverse=reverse, a...]
    all_gather x12 -> x0, blocking collectives: 99.1 us -> none  [prefix(): gathered = jax.tree.map(lambda a: lax.all_gather(a, axis), part)]
    slice x187 -> x1, local copies, waits for them, and re-layouts: 87.6 us -> 0.51 us  [shards(): direction = ratio[0, 0] * prev_direction - gradient]
    psum x2 -> x0, blocking collectives: 33.5 us -> none  [the longest x1 30.1 us: shards(): lax.psum((jnp.sum(gradient * (gradient - prev_gradient)), jnp.sum(prev_gr...]
    pallas_call x0 -> x1, Pallas kernels: none -> 29.5 us  [shards(): pl.pallas_call(functools.partial(kernel, (n_gx, n_gy, n_gz)), out_shape=(...]
    scatter-add x2 -> x0, other arithmetic: 6.51 us -> none  [the longest x1 3.26 us: shards(): back_north = jnp.zeros((cell_count,), jnp.float32).at[located].add(sines...]
    gather x2 -> x0, local copies, waits for them, and re-layouts: 6.29 us -> none  [shards(): projected = cosine * flat_east[located] + sines * flat_north[located]]
where the time goes in v1:
time: 40.5 us; the launch traced here: 40.1 us
  Pallas kernels  29.5 us (73%)
  local copies, waits for them, and re-layouts  8.64 us (21%)
  other arithmetic  1.34 us (3%)
  between operations  0.66 us (2%)
    pallas_call x1, Pallas kernels, shards(): pl.pallas_call(functools.partial(kernel, (n_gx, n_gy, n_gz)), out_shape=(...  29.5 us
    unnamed x22, local copies, waits for them, and re-layouts  8.13 us
    sub x1, other arithmetic, shards(): direction = ratio[0, 0] * prev_direction - gradient  1.34 us

profile of v1, /device:TPU:0, one launch (start us, length us, event | category | flops | bytes accessed | tf_op | source)
XLA Modules:
  0.0 40.1 jit_solution(2351606105866136206)
XLA Ops:
  0.6 0.0 copy-start
  0.6 0.9 %copy-done = f32[20,8,256]{2,1,0:T(8,128)S(1)} copy-done((f32[20,8,256]{2,1,0:T(8,128)S(1)}, f32[20,8,256]{2,1,0:T(8,128)}, u32[]{:S(2)}) %copy-start) | copy-done | bytes 163864
  1.6 0.0 copy-start.1
  1.6 0.9 %copy-done.1 = bf16[2,20,8,256]{3,2,1,0:T(8,128)(2,1)S(1)} copy-done((bf16[2,20,8,256]{3,2,1,0:T(8,128)(2,1)S(1)}, bf16[2,20,8,256]{3,2,1,0:T(8,128)(2,1)}, u32[]{:S(2)}) %copy-start.1) | copy-done | bytes 163864
  2.5 0.0 copy-start.2
  2.5 0.9 %copy-done.2 = f32[20,8,256]{2,1,0:T(8,128)S(1)} copy-done((f32[20,8,256]{2,1,0:T(8,128)S(1)}, f32[20,8,256]{2,1,0:T(8,128)}, u32[]{:S(2)}) %copy-start.2) | copy-done | bytes 163864
  3.4 0.0 copy-start.3
  3.4 0.7 %copy-done.3 = f32[8,256]{1,0:T(8,128)S(1)} copy-done((f32[8,256]{1,0:T(8,128)S(1)}, f32[8,256]{1,0:T(8,128)}, u32[]{:S(2)}) %copy-start.3) | copy-done | bytes 8216
  4.1 0.0 copy-start.4
  4.1 0.7 %copy-done.4 = f32[8,256]{1,0:T(8,128)S(1)} copy-done((f32[8,256]{1,0:T(8,128)S(1)}, f32[8,256]{1,0:T(8,128)}, u32[]{:S(2)}) %copy-start.4) | copy-done | bytes 8216
  4.8 0.0 copy-start.5
  4.8 0.7 %copy-done.5 = s32[1,1,512]{2,1,0:T(1,128)S(1)} copy-done((s32[1,1,512]{2,1,0:T(1,128)S(1)}, s32[1,1,512]{2,1,0:T(1,128)}, u32[]{:S(2)}) %copy-start.5) | copy-done | bytes 2072
  5.5 0.0 copy-start.6
  5.5 0.7 %copy-done.6 = s32[1,1,512]{2,1,0:T(1,128)S(1)} copy-done((s32[1,1,512]{2,1,0:T(1,128)S(1)}, s32[1,1,512]{2,1,0:T(1,128)}, u32[]{:S(2)}) %copy-start.6) | copy-done | bytes 2072
  6.1 0.0 copy-start.7
  6.1 0.7 %copy-done.7 = f32[1,1,512]{2,1,0:T(1,128)S(1)} copy-done((f32[1,1,512]{2,1,0:T(1,128)S(1)}, f32[1,1,512]{2,1,0:T(1,128)}, u32[]{:S(2)}) %copy-start.7) | copy-done | bytes 2072
  6.8 0.0 copy-start.8
  6.8 0.7 %copy-done.8 = f32[1,1,512]{2,1,0:T(1,128)S(1)} copy-done((f32[1,1,512]{2,1,0:T(1,128)S(1)}, f32[1,1,512]{2,1,0:T(1,128)}, u32[]{:S(2)}) %copy-start.8) | copy-done | bytes 2072
  7.5 29.5 %shard_map.121 = (f32[20,8,256]{2,1,0:T(8,128)S(1)}, f32[2,8,256]{2,1,0:T(8,128)S(1)}, f32[8,128]{1,0:T(8,128)S(1)}) custom-call(f32[20,8,256]{2,1,0:T(8,128)S(1)} %copy-done, bf16[2,20,8,256]{3,2,1,0:T(8,128)(2,1)S(1)} %copy-done.1, f32[8,256]{1,0:T(8,128)S(1)} %copy-done.3, f32[8,256]{1,0:T(8,128)S(1)} %copy-done.4, s32[1,1,512]{2,1,0:T(1,128)S(1)} %copy-done.5, ...), custom_call_target="tpu_custom_call" | custom-call | tf_op jit(solution)/shard_map/pallas_call | solution.py:409
  37.0 0.5 %slice.3 = f32[1,1]{1,0:T(1,128)} slice(f32[8,128]{1,0:T(8,128)S(1)} %get-tuple-element.7), slice={[0:1], [0:1]} | slice | bytes 8 | tf_op jit(solution)/shard_map/slice | solution.py:441
  37.5 0.0 copy-done.9
  37.5 1.3 %multiply_subtract_fusion = f32[20,8,256]{2,1,0:T(8,128)} fusion(f32[20,8,256]{2,1,0:T(8,128)S(1)} %get-tuple-element.12, f32[20,8,256]{2,1,0:T(8,128)S(1)} %copy-done.9, f32[]{:T(128)} %bitcast), kind=kLoop, calls=%fused_computation | loop fusion | flops 81920 | bytes 491524 | tf_op jit(solution)/shard_map/sub | solution.py:441
  38.8 0.7 %copy.15 = f32[20,8,256]{2,1,0:T(8,128)} copy(f32[20,8,256]{2,1,0:T(8,128)S(1)} %get-tuple-element.12) | data formatting | bytes 327680
  39.5 0.6 %copy.16 = f32[2,8,256]{2,1,0:T(8,128)} copy(f32[2,8,256]{2,1,0:T(8,128)S(1)} %get-tuple-element.14) | data formatting | bytes 32768
  (1 shorter events, 0.0 us)
Async XLA Ops:
  0.6 0.9 %copy-start = (f32[20,8,256]{2,1,0:T(8,128)S(1)}, f32[20,8,256]{2,1,0:T(8,128)}, u32[]{:S(2)}) copy-start(f32[20,8,256]{2,1,0:T(8,128)} %controls_h.1) | copy-start | bytes 491524
  1.6 0.9 %copy-start.1 = (bf16[2,20,8,256]{3,2,1,0:T(8,128)(2,1)S(1)}, bf16[2,20,8,256]{3,2,1,0:T(8,128)(2,1)}, u32[]{:S(2)}) copy-start(bf16[2,20,8,256]{3,2,1,0:T(8,128)(2,1)} %anomalies_h.1) | copy-start | bytes 491524
  2.5 0.9 %copy-start.2 = (f32[20,8,256]{2,1,0:T(8,128)S(1)}, f32[20,8,256]{2,1,0:T(8,128)}, u32[]{:S(2)}) copy-start(f32[20,8,256]{2,1,0:T(8,128)} %prev_h.1) | copy-start | bytes 491524
  3.4 0.7 %copy-start.3 = (f32[8,256]{1,0:T(8,128)S(1)}, f32[8,256]{1,0:T(8,128)}, u32[]{:S(2)}) copy-start(f32[8,256]{1,0:T(8,128)} %x_rates_h.1) | copy-start | bytes 24580
  4.1 0.7 %copy-start.4 = (f32[8,256]{1,0:T(8,128)S(1)}, f32[8,256]{1,0:T(8,128)}, u32[]{:S(2)}) copy-start(f32[8,256]{1,0:T(8,128)} %y_rates_h.1) | copy-start | bytes 24580
  4.8 0.7 %copy-start.5 = (s32[1,1,512]{2,1,0:T(1,128)S(1)}, s32[1,1,512]{2,1,0:T(1,128)}, u32[]{:S(2)}) copy-start(s32[1,1,512]{2,1,0:T(1,128)} %cells_h.1) | copy-start | bytes 6148
  5.5 0.7 %copy-start.6 = (s32[1,1,512]{2,1,0:T(1,128)S(1)}, s32[1,1,512]{2,1,0:T(1,128)}, u32[]{:S(2)}) copy-start(s32[1,1,512]{2,1,0:T(1,128)} %codes_h.1) | copy-start | bytes 6148
  6.1 0.7 %copy-start.7 = (f32[1,1,512]{2,1,0:T(1,128)S(1)}, f32[1,1,512]{2,1,0:T(1,128)}, u32[]{:S(2)}) copy-start(f32[1,1,512]{2,1,0:T(1,128)} %values_h.1) | copy-start | bytes 6148
  6.8 0.7 %copy-start.8 = (f32[1,1,512]{2,1,0:T(1,128)S(1)}, f32[1,1,512]{2,1,0:T(1,128)}, u32[]{:S(2)}) copy-start(f32[1,1,512]{2,1,0:T(1,128)} %weights_h.1) | copy-start | bytes 6148
  7.5 30.0 %copy-start.9 = (f32[20,8,256]{2,1,0:T(8,128)S(1)}, f32[20,8,256]{2,1,0:T(8,128)}, u32[]{:S(2)}) copy-start(f32[20,8,256]{2,1,0:T(8,128)} %param.19) | copy-start | bytes 491524

commit v2 on v1

--- a/solution.py
+++ b/solution.py
@@ -10,7 +10,7 @@
 
 NDIR = 72
 LANES = 128
-ROWS = 8
+VMEM_BYTES = 63 * 1024 * 1024
 MESH = pl.DeviceIdType.MESH
 
 
@@ -65,10 +65,10 @@
 
 def kernel(
     sizes,
-    controls_h, anomalies_h, x_rates_h, y_rates_h, cells_h, codes_h, values_h, weights_h, prev_h,
-    gradient_h, increment_h, ratio_ref,
-    controls, anomalies, x_rates, y_rates, cells, codes, values, weights, prev,
-    gradient, increment, work, enter, slots_x, slots_y, slots_z, slots_s,
+    controls_h, anomalies_h, x_rates_h, y_rates_h, cells_h, codes_h, values_h, weights_h, prev_h, old_h,
+    gradient_h, direction_h, increment_h,
+    controls, anomalies, x_rates, y_rates, cells, codes, values, weights, prev, old,
+    gradient, direction, increment, work, enter, slots_x, slots_y, slots_z, slots_s, of_column,
     load_sem, store_sem, send_x, recv_x, send_y, recv_y, send_z, recv_z, send_s, recv_s,
 ):
     n_gx, n_gy, n_gz = sizes
@@ -79,26 +79,30 @@
     parts = [slice(at, at + LANES) for at in range(0, columns, LANES)]
     spread = 1.0 / math.sqrt(members * n_gz - 1)
 
-    def place_of(peer):
-        return {"gx": peer // (n_gy * n_gz), "gy": peer // n_gz % n_gy, "gz": peer % n_gz}
+    near = [(lax.rem(gy + b, n_gy), lax.rem(gz + c, n_gz)) for b in range(n_gy) for c in range(n_gz)]
 
     def each_peer(body):
-        if total <= 32:
-            for off in range(1, total):
-                body(lax.rem(me + off, total))
+        def visit(x, others):
+            for y, z in others:
+                body((x * n_gy + y) * n_gz + z, {"gx": x, "gy": y, "gz": z})
+
+        visit(gx, near[1:])
+        if n_gx <= 4:
+            for off in range(1, n_gx):
+                visit(lax.rem(gx + off, n_gx), near)
         else:
-            lax.fori_loop(1, total, lambda off, c: (body(lax.rem(me + off, total)), c)[1], 0)
+            lax.fori_loop(1, n_gx, lambda off, c: (visit(lax.rem(gx + off, n_gx), near), c)[1], 0)
 
     barrier = pltpu.get_barrier_semaphore()
-    each_peer(lambda peer: pl.semaphore_signal(
-        barrier, inc=1, device_id=place_of(peer), device_id_type=MESH))
+    each_peer(lambda index, place: pl.semaphore_signal(
+        barrier, inc=1, device_id=place, device_id_type=MESH))
 
     loads = [
         pltpu.make_async_copy(src, dst, load_sem.at[i])
         for i, (src, dst) in enumerate((
             (x_rates_h, x_rates), (controls_h, controls), (y_rates_h, y_rates),
             (anomalies_h, anomalies), (cells_h, cells), (codes_h, codes), (values_h, values),
-            (weights_h, weights), (prev_h, prev)))
+            (weights_h, weights), (prev_h, prev), (old_h, old)))
     ]
     for load in loads:
         load.start()
@@ -112,16 +116,20 @@
             tile = jnp.where(row_at == s, rolled(block, s - from_row, 0), tile)
         return tile
 
-    def local_x(leading, lines, turn):
+    def local_x(leading, lines, turn, beyond=None):
         outs = []
-        for part, line, lead in zip(parts, lines, leading):
+        for at, (part, line, lead) in enumerate(zip(parts, lines, leading)):
             inward, outward = line.local(lead)
             ends = [inward[k] for k in range(members)] + [line.onward[0]]
             heads = [outward[k] for k in range(members)] + [line.echo[0]]
             for group in range(slots_x.shape[3] // rows):
                 here = pl.ds(group * rows, rows)
-                slots_x[turn, gx, 0, here, part] = pack_rows(ends, rows - 1, group)
-                slots_x[turn, gx, 1, here, part] = pack_rows(heads, 0, group)
+                end = pack_rows(ends, rows - 1, group)
+                head = pack_rows(heads, 0, group)
+                if beyond is not None:
+                    head = head + beyond[at] * end
+                slots_x[turn, gx, 0, here, part] = end
+                slots_x[turn, gx, 1, here, part] = head
             outs.append(outward)
         return outs
 
@@ -131,44 +139,75 @@
             send_sem=send_x.at[turn, kind, peer], recv_sem=recv_x.at[turn, kind, source],
             device_id={"gx": peer}, device_id_type=MESH)
 
-    def start_x(turn):
+    def outgoing_x(turn, act):
         for off in range(1, n_gx):
             peer = lax.rem(gx + off, n_gx)
-            copy_x(turn, 0, gx, peer).start()
+
+            @pl.when(gx < n_gx - 1 if turn == 0 else peer > gx)
+            def _():
+                act(copy_x(turn, 0, gx, peer))
 
             @pl.when(peer < gx)
             def _():
-                copy_x(turn, 1, gx, peer).start()
-
-    def finish_x(turn, lines, outs):
+                act(copy_x(turn, 1, gx, peer))
+
+    def incoming_x(turn):
         for off in range(1, n_gx):
             source = lax.rem(gx + off, n_gx)
-            copy_x(turn, 0, source, source).wait_recv()
+
+            @pl.when(source < n_gx - 1 if turn == 0 else source < gx)
+            def _():
+                copy_x(turn, 0, source, source).wait_recv()
 
             @pl.when(source > gx)
             def _():
                 copy_x(turn, 1, source, source).wait_recv()
 
+    def states_x(turn, part):
+        state = jnp.zeros((slots_x.shape[3], LANES), jnp.float32)
+        states = [state]
+        mine = state
+        for t in range(n_gx - 1):
+            through = slots_x[0, t, 0, members:members + 1, part]
+            state = through * state + slots_x[turn, t, 0, :, part]
+            states.append(state)
+            mine = jnp.where(gx == t + 1, state, mine)
+        return states, mine
+
+    def backward_x(turn, part, states):
+        state = jnp.zeros((slots_x.shape[3], LANES), jnp.float32)
+        mine = state
+        for t in range(n_gx - 1, 0, -1):
+            if t < n_gx - 1:
+                state = slots_x[0, t, 0, members:members + 1, part] * state
+            state = state + slots_x[turn, t, 1, :, part]
+            if states is not None:
+                state = state + slots_x[0, t, 1, members:members + 1, part] * states[t]
+            mine = jnp.where(gx == t - 1, state, mine)
+        return mine
+
+    def response_x(part):
+        factor = jnp.zeros((1, LANES), jnp.float32)
+        mine = factor
+        for t in range(n_gx - 1, 0, -1):
+            if t < n_gx - 1:
+                through = slots_x[0, t, 0, members:members + 1, part]
+                factor = through * through * factor
+            factor = factor + slots_x[0, t, 1, members:members + 1, part]
+            mine = jnp.where(gx == t - 1, factor, mine)
+        return mine
+
+    def finish_x(turn, lines, outs, responses=None):
+        incoming_x(turn)
         results = []
-        for part, line, outward in zip(parts, lines, outs):
-            ends = [slots_x[turn, t, 0, :, part] for t in range(n_gx)]
-            heads = [slots_x[turn, t, 1, :, part] for t in range(n_gx)]
-            through = [v[members:members + 1] for v in ends]
-            echoes = [v[members:members + 1] for v in heads]
-            state = jnp.zeros_like(ends[0])
-            states = [state]
-            mine = state
-            for t in range(n_gx - 1):
-                state = through[t] * state + ends[t]
-                states.append(state)
-                mine = jnp.where(gx == t + 1, state, mine)
+        for at, (part, line, outward) in enumerate(zip(parts, lines, outs)):
+            states, mine = states_x(turn, part)
             enter[0, :, part] = mine
-            state = jnp.zeros_like(ends[0])
-            mine = state
-            for t in range(n_gx - 1, 0, -1):
-                state = through[t] * state + heads[t] + echoes[t] * states[t]
-                mine = jnp.where(gx == t - 1, state, mine)
-            enter[1, :, part] = mine
+            if responses is None:
+                enter[1, :, part] = backward_x(turn, part, states)
+            else:
+                leaving = slots_x[0, gx, 0, members:members + 1, part] * mine + slots_x[turn, gx, 0, :, part]
+                enter[1, :, part] = backward_x(turn, part, None) + responses[at] * leaving
             for k in range(members):
                 first = jnp.broadcast_to(enter[0, k:k + 1, part], (rows, LANES))
                 second = jnp.broadcast_to(enter[1, k:k + 1, part], (rows, LANES))
@@ -252,7 +291,7 @@
     loads[1].wait()
     held = local_x([line.scales * controls[:, :, part] for part, line in zip(parts, lines_x)], lines_x, 0)
     pl.semaphore_wait(barrier, total - 1)
-    start_x(0)
+    outgoing_x(0, lambda copy: copy.start())
 
     loads[2].wait()
     lines_y = [Line(y_rates[:, part][None], 2) for part in parts]
@@ -278,8 +317,9 @@
     bearing = codes[0].astype(jnp.float32) * (2.0 * math.pi / NDIR)
     cosine = jnp.cos(bearing)
     sine = jnp.sin(bearing)
-    at_column = (lax.broadcasted_iota(jnp.int32, (columns, n_obs), 0) == cell_column).astype(
-        jnp.float32).astype(jnp.bfloat16)
+    hit = (lax.broadcasted_iota(jnp.int32, (columns, n_obs), 0) == cell_column).astype(jnp.float32)
+    at_column = hit.astype(jnp.bfloat16)
+    of_column[...] = hit.T.astype(jnp.bfloat16)
     in_row = lax.broadcasted_iota(jnp.int32, (rows, n_obs), 0) == cell_row
     toward = jnp.concatenate([jnp.where(in_row, cosine, 0.0), jnp.where(in_row, sine, 0.0)], axis=0)
     before = prev[...]
@@ -289,6 +329,8 @@
 
     held = local_y([line.scales * v for line, v in zip(lines_y, filtered)], lines_y, factors_y, 0)
     start_y(0)
+    responses = [response_x(part) for part in parts]
+    beyond = [line.onward[0, rows - 1:] * response for line, response in zip(lines_x, responses)]
     filtered = finish_y(0, lines_y, factors_y, held)
 
     for c in range(2):
@@ -323,9 +365,8 @@
     lifted = lifted[:2 * rows] + (lifted[2 * rows:4 * rows] + lifted[4 * rows:])
     projected = jnp.sum(lifted * toward, axis=0, keepdims=True)
     misfit = weights[0] * (projected - values[0])
-    back = lax.dot_general(
-        split_three(toward * misfit), at_column, (((1,), (1,)), ((), ())),
-        preferred_element_type=jnp.float32)
+    back = jnp.dot(
+        split_three(toward * misfit), of_column[...], preferred_element_type=jnp.float32)
     back = (back[:2 * rows] + (back[2 * rows:4 * rows] + back[4 * rows:])) * spread
 
     leading = []
@@ -342,9 +383,9 @@
         for k in range(members):
             work[k, :, part] = scale * field[k]
         leading.append(work[:, :, part])
-    held = local_x(leading, lines_x, 1)
-    start_x(1)
-    smoothed = finish_x(1, lines_x, held)
+    held = local_x(leading, lines_x, 1, beyond)
+    outgoing_x(1, lambda copy: copy.start())
+    smoothed = finish_x(1, lines_x, held, responses)
     numerator = jnp.zeros((rows, LANES), jnp.float32)
     for part, line, field in zip(parts, lines_x, smoothed):
         new = controls[:, :, part] + line.scales / line.rates * field
@@ -359,33 +400,39 @@
     slots_s[me, 0:1] = jnp.sum(numerator, axis=0, keepdims=True)
     slots_s[me, 1:2] = halves
 
-    def copy_s(source, peer):
+    def copy_s(source, peer, place):
         return pltpu.make_async_remote_copy(
             src_ref=slots_s.at[source], dst_ref=slots_s.at[source],
             send_sem=send_s.at[peer], recv_sem=recv_s.at[source],
-            device_id=place_of(peer), device_id_type=MESH)
-
-    each_peer(lambda peer: copy_s(me, peer).start())
-    each_peer(lambda peer: copy_s(peer, peer).wait_recv())
+            device_id=place, device_id_type=MESH)
+
+    each_peer(lambda peer, place: copy_s(me, peer, place).start())
+    each_peer(lambda peer, place: copy_s(peer, peer, place).wait_recv())
     sums = jnp.sum(jnp.sum(slots_s[...], axis=0), axis=1, keepdims=True)
-    ratio_ref[...] = jnp.broadcast_to(sums[0:1] / sums[1:2], ratio_ref.shape)
-
-    each_peer(lambda peer: copy_s(me, peer).wait_send())
+    direction[...] = (sums[0:1] / sums[1:2])[None] * old[...] - gradient[...]
+    store_direction = pltpu.make_async_copy(direction, direction_h, store_sem.at[2])
+    store_direction.start()
+
+    each_peer(lambda peer, place: copy_s(me, peer, place).wait_send())
     for turn in range(2):
-        for off in range(1, n_gx):
-            peer = lax.rem(gx + off, n_gx)
-            copy_x(turn, 0, gx, peer).wait_send()
-
-            @pl.when(peer < gx)
-            def _():
-                copy_x(turn, 1, gx, peer).wait_send()
-
+        outgoing_x(turn, lambda copy: copy.wait_send())
         for off in range(1, n_gy):
             copy_y(turn, gy, lax.rem(gy + off, n_gy)).wait_send()
     for off in range(1, n_gz):
         copy_z(gz, lax.rem(gz + off, n_gz)).wait_send()
     store_increment.wait()
     store_gradient.wait()
+    store_direction.wait()
+
+
+def results_kernel(*refs):
+    count = len(refs) // 2
+    sems = refs[-1]
+    copies = [pltpu.make_async_copy(refs[i], refs[count + i], sems.at[i]) for i in range(count)]
+    for copy in copies:
+        copy.start()
+    for copy in copies:
+        copy.wait()
 
 
 def shards(
@@ -404,22 +451,20 @@
     total = n_gx * n_gy * n_gz
     members, rows, columns = controls.shape
     packed = -(-(members + 1) // rows) * rows
-    args = (controls, anomalies, x_rates, y_rates, obs_cells, obs_codes, obs_values, obs_weights, prev_gradient)
+    args = (controls, anomalies, x_rates, y_rates, obs_cells, obs_codes, obs_values, obs_weights, prev_gradient,
+            prev_direction)
     dma = pltpu.SemaphoreType.DMA
-    gradient, increment, ratio = pl.pallas_call(
+    anywhere = pl.BlockSpec(memory_space=pl.ANY)
+    results = tuple(
+        jax.ShapeDtypeStruct(shape, jnp.float32)
+        for shape in (controls.shape, controls.shape, (2, rows, columns)))
+    held = pl.pallas_call(
         functools.partial(kernel, (n_gx, n_gy, n_gz)),
-        out_shape=(
-            jax.ShapeDtypeStruct(controls.shape, jnp.float32),
-            jax.ShapeDtypeStruct((2, rows, columns), jnp.float32),
-            jax.ShapeDtypeStruct((ROWS, LANES), jnp.float32),
-        ),
-        in_specs=[pl.BlockSpec(memory_space=pl.ANY)] * len(args),
-        out_specs=(
-            pl.BlockSpec(memory_space=pl.ANY),
-            pl.BlockSpec(memory_space=pl.ANY),
-            pl.BlockSpec(memory_space=pltpu.VMEM),
-        ),
+        out_shape=results,
+        in_specs=[anywhere] * len(args),
+        out_specs=(anywhere,) * len(results),
         scratch_shapes=[pltpu.VMEM(a.shape, a.dtype) for a in args] + [
+            pltpu.VMEM(controls.shape, jnp.float32),
             pltpu.VMEM(controls.shape, jnp.float32),
             pltpu.VMEM((2, rows, columns), jnp.float32),
             pltpu.VMEM(controls.shape, jnp.float32),
@@ -428,18 +473,25 @@
             pltpu.VMEM((2, n_gy, 2, rows, LANES), jnp.float32),
             pltpu.VMEM((n_gz, 2, rows, columns), jnp.float32),
             pltpu.VMEM((total, 2, LANES), jnp.float32),
-            dma((len(args),)), dma((2,)),
+            pltpu.VMEM((columns, obs_cells.shape[-1])[::-1], jnp.bfloat16),
+            dma((len(args),)), dma((3,)),
             dma((2, 2, n_gx)), dma((2, 2, n_gx)),
             dma((2, n_gy)), dma((2, n_gy)),
             dma((n_gz,)), dma((n_gz,)),
             dma((total,)), dma((total,)),
         ],
         compiler_params=pltpu.CompilerParams(
-            collective_id=0, has_side_effects=True, vmem_limit_bytes=40 * 1024 * 1024
+            collective_id=0, has_side_effects=True, vmem_limit_bytes=VMEM_BYTES
         ),
     )(*args)
-    direction = ratio[0, 0] * prev_direction - gradient
-    return (gradient, direction, increment)
+    return pl.pallas_call(
+        results_kernel,
+        out_shape=results,
+        in_specs=[anywhere] * len(results),
+        out_specs=(anywhere,) * len(results),
+        scratch_shapes=[dma((len(results),))],
+        compiler_params=pltpu.CompilerParams(vmem_limit_bytes=VMEM_BYTES),
+    )(*held)
 
 
 def solution(mesh):

time: 40.5 us -> 41.3 us (1.020)
  Pallas kernels: 29.5 us -> 40.5 us
  local copies, waits for them, and re-layouts: 8.64 us -> 0 us
  other arithmetic: 1.34 us -> 0 us
    pallas_call x1 -> x2, Pallas kernels: 29.5 us -> 40.5 us  [the longest x1 28.9 us: shards(): pl.pallas_call(functools.partial(kernel, (n_gx, n_gy, n_gz)), out_shape=r...]
    unnamed x22 -> x0, local copies, waits for them, and re-layouts: 8.13 us -> none
    sub x1 -> x0, other arithmetic: 1.34 us -> none  [shards(): direction = ratio[0, 0] * prev_direction - gradient]
    slice x1 -> x0, local copies, waits for them, and re-layouts: 0.51 us -> none  [shards(): direction = ratio[0, 0] * prev_direction - gradient]
where the time goes in v2:
time: 41.3 us; the launch traced here: 41.1 us
  Pallas kernels  40.5 us (98%)
  between operations  0.64 us (2%)
    pallas_call x1, Pallas kernels, shards(): pl.pallas_call(functools.partial(kernel, (n_gx, n_gy, n_gz)), out_shape=r...  28.9 us
    pallas_call x1, Pallas kernels, shards(): pl.pallas_call(results_kernel, out_shape=results, in_specs=[anywhere] * l...  11.6 us

profile of v2, /device:TPU:0, one launch (start us, length us, event | category | flops | bytes accessed | tf_op | source)
XLA Modules:
  0.0 41.1 jit_solution(9750026991154771678)
XLA Ops:
  0.6 28.9 %shard_map.121 = (f32[20,8,256]{2,1,0:T(8,128)}, f32[20,8,256]{2,1,0:T(8,128)}, f32[2,8,256]{2,1,0:T(8,128)}) custom-call(f32[20,8,256]{2,1,0:T(8,128)} %controls_h.1, bf16[2,20,8,256]{3,2,1,0:T(8,128)(2,1)} %anomalies_h.1, f32[8,256]{1,0:T(8,128)} %x_rates_h.1, f32[8,256]{1,0:T(8,128)} %y_rates_h.1, s32[1,1,512]{2,1,0:T(1,128)} %cells_h.1, ...), custom_call_target="tpu_custom_call" | custom-call | tf_op jit(solution)/shard_map/pallas_call | solution.py:461
  29.6 11.6 %shard_map.122 = (f32[20,8,256]{2,1,0:T(8,128)}, f32[20,8,256]{2,1,0:T(8,128)}, f32[2,8,256]{2,1,0:T(8,128)}) custom-call(f32[20,8,256]{2,1,0:T(8,128)} %get-tuple-element.6.refs_0_, f32[20,8,256]{2,1,0:T(8,128)} %get-tuple-element.7.refs_1_, f32[2,8,256]{2,1,0:T(8,128)} %get-tuple-element.8.refs_2_), custom_call_target="tpu_custom_call" | custom-call | tf_op jit(solution)/shard_map/pallas_call | solution.py:487

commit v3 on v2

--- a/solution.py
+++ b/solution.py
@@ -68,7 +68,7 @@
     controls_h, anomalies_h, x_rates_h, y_rates_h, cells_h, codes_h, values_h, weights_h, prev_h, old_h,
     gradient_h, direction_h, increment_h,
     controls, anomalies, x_rates, y_rates, cells, codes, values, weights, prev, old,
-    gradient, direction, increment, work, enter, slots_x, slots_y, slots_z, slots_s, of_column,
+    gradient, direction, increment, work, enter, slots_x, slots_y, slots_z, slots_a, slots_s, of_column,
     load_sem, store_sem, send_x, recv_x, send_y, recv_y, send_z, recv_z, send_s, recv_s,
 ):
     n_gx, n_gy, n_gz = sizes
@@ -224,67 +224,62 @@
     def across(tile, lane):
         return jnp.broadcast_to(tile[:, lane:lane + 1], (rows, LANES))
 
-    def local_y(leading, lines, factors, turn):
-        outs, ends, heads = [], [], []
-        for line, lead in zip(lines, leading):
+    def local_y(leading, lines, turn):
+        outs = []
+        for s, (line, lead) in enumerate(zip(lines, leading)):
             inward, outward = line.local(lead)
-            ends.append(pack_lanes(inward, LANES - 1))
-            heads.append(pack_lanes(outward, 0))
+            slots_y[turn, gy, gz, s, 0] = jnp.where(
+                lane_at == members, across(line.onward[0], LANES - 1), pack_lanes(inward, LANES - 1))
+            slots_y[turn, gy, gz, s, 1] = jnp.where(
+                lane_at == members, across(line.echo[0], 0), pack_lanes(outward, 0))
             outs.append(outward)
-        through, echoes, whole_through, whole_echo = factors
+        return outs
+
+    def each_y(turn, act):
+        for y, z in near[1:] if turn == 0 else [near[b * n_gz] for b in range(1, n_gy)]:
+            act(y, z)
+
+    def copy_y(turn, source, peer):
+        slot = (turn, *source)
+        return pltpu.make_async_remote_copy(
+            src_ref=slots_y.at[slot], dst_ref=slots_y.at[slot],
+            send_sem=send_y.at[turn, *peer], recv_sem=recv_y.at[turn, *source],
+            device_id={"gy": peer[0], "gz": peer[1]}, device_id_type=MESH)
+
+    def start_y(turn):
+        each_y(turn, lambda *peer: copy_y(turn, (gy, gz), peer).start())
+
+    def entering_y(turn, z):
+        chain = [(t, s) for t in range(n_gy) for s in range(len(parts))]
         state = jnp.zeros((rows, LANES), jnp.float32)
         states = []
-        for a, f in zip(through, ends):
+        firsts = [state] * len(parts)
+        for t, s in chain:
             states.append(state)
-            state = a * state + f
-        back = jnp.zeros((rows, LANES), jnp.float32)
-        for a, c, b, h in reversed(list(zip(through, echoes, heads, states))):
-            back = a * back + b + c * h
-        slots_y[turn, gy, 0] = jnp.where(lane_at == members, whole_through, state)
-        slots_y[turn, gy, 1] = jnp.where(lane_at == members, whole_echo, back)
-        return outs, ends, heads
-
-    def copy_y(turn, source, peer):
+            firsts[s] = state if t == 0 else jnp.where(gy == t, state, firsts[s])
+            tile = slots_y[turn, t, z, s, 0]
+            state = across(tile, members) * state + tile
+        state = jnp.zeros((rows, LANES), jnp.float32)
+        seconds = [state] * len(parts)
+        for (t, s), entered in reversed(list(zip(chain, states))):
+            seconds[s] = state if t == n_gy - 1 else jnp.where(gy == t, state, seconds[s])
+            tile = slots_y[turn, t, z, s, 1]
+            state = across(slots_y[turn, t, z, s, 0], members) * state + tile + across(tile, members) * entered
+        return firsts, seconds
+
+    def copy_z(source, peer):
         return pltpu.make_async_remote_copy(
-            src_ref=slots_y.at[turn, source], dst_ref=slots_y.at[turn, source],
-            send_sem=send_y.at[turn, peer], recv_sem=recv_y.at[turn, source],
-            device_id={"gy": peer}, device_id_type=MESH)
-
-    def start_y(turn):
-        for off in range(1, n_gy):
-            copy_y(turn, gy, lax.rem(gy + off, n_gy)).start()
-
-    def finish_y(turn, lines, factors, held):
-        outs, ends, heads = held
-        through, echoes, _, _ = factors
-        for off in range(1, n_gy):
-            source = lax.rem(gy + off, n_gy)
-            copy_y(turn, source, source).wait_recv()
-        state = jnp.zeros((rows, LANES), jnp.float32)
-        states = [state]
-        first = state
-        for t in range(n_gy - 1):
-            tile = slots_y[turn, t, 0]
-            state = across(tile, members) * state + tile
-            states.append(state)
-            first = jnp.where(gy == t + 1, state, first)
-        state = jnp.zeros((rows, LANES), jnp.float32)
-        second = state
-        for t in range(n_gy - 1, 0, -1):
-            tile = slots_y[turn, t, 1]
-            state = across(slots_y[turn, t, 0], members) * state + tile + across(tile, members) * states[t]
-            second = jnp.where(gy == t - 1, state, second)
-        firsts, seconds = [], []
-        for a, f in zip(through, ends):
-            firsts.append(first)
-            first = a * first + f
-        for a, c, b, h in reversed(list(zip(through, echoes, heads, firsts))):
-            seconds.insert(0, second)
-            second = a * second + b + c * h
-        return [
-            [outward[k] + line.echo[0] * across(h, k) + line.back[0] * across(b, k) for k in range(members)]
-            for line, outward, h, b in zip(lines, outs, firsts, seconds)
-        ]
+            src_ref=slots_z.at[source], dst_ref=slots_z.at[source],
+            send_sem=send_z.at[0, peer], recv_sem=recv_z.at[0, source],
+            device_id={"gz": peer}, device_id_type=MESH)
+
+    def copy_a(source, peer):
+        return pltpu.make_async_remote_copy(
+            src_ref=slots_a.at[source], dst_ref=slots_a.at[source],
+            send_sem=send_z.at[1, peer], recv_sem=recv_z.at[1, source],
+            device_id={"gz": peer}, device_id_type=MESH)
+
+    other_z = [lax.rem(gz + off, n_gz) for off in range(1, n_gz)]
 
     loads[0].wait()
     lines_x = [Line(x_rates[:, part][None], 1) for part in parts]
@@ -295,20 +290,11 @@
 
     loads[2].wait()
     lines_y = [Line(y_rates[:, part][None], 2) for part in parts]
-    through_y = [across(line.onward[0], LANES - 1) for line in lines_y]
-    echoes_y = [across(line.echo[0], 0) for line in lines_y]
-    whole_through = jnp.ones((rows, LANES), jnp.float32)
-    reach = []
-    for a in through_y:
-        reach.append(whole_through)
-        whole_through = whole_through * a
-    whole_echo = jnp.zeros((rows, LANES), jnp.float32)
-    for a, c, h in reversed(list(zip(through_y, echoes_y, reach))):
-        whole_echo = a * whole_echo + c * h
-    factors_y = (through_y, echoes_y, whole_through, whole_echo)
-
     for load in loads[3:]:
         load.wait()
+    slots_a[gz] = anomalies[...].astype(jnp.float32)
+    for z in other_z:
+        copy_a(gz, z).start()
     n_obs = cells.shape[-1]
     cell = cells[0]
     bits = columns.bit_length() - 1
@@ -327,34 +313,32 @@
 
     filtered = finish_x(0, lines_x, held)
 
-    held = local_y([line.scales * v for line, v in zip(lines_y, filtered)], lines_y, factors_y, 0)
+    outs = local_y([line.scales * v for line, v in zip(lines_y, filtered)], lines_y, 0)
     start_y(0)
+    for c in range(2):
+        for part, field in zip(parts, outs):
+            slots_z[gz, c, :, part] = jnp.sum(slots_a[gz, c, :, :, part] * field, axis=0)
+    for z in other_z:
+        copy_z(gz, z).start()
     responses = [response_x(part) for part in parts]
     beyond = [line.onward[0, rows - 1:] * response for line, response in zip(lines_x, responses)]
-    filtered = finish_y(0, lines_y, factors_y, held)
-
-    for c in range(2):
-        for part, field in zip(parts, filtered):
-            summed = jnp.zeros((rows, LANES), jnp.float32)
+    for z in other_z:
+        copy_a(z, z).wait_recv()
+    each_y(0, lambda *source: copy_y(0, source, source).wait_recv())
+    for z in other_z:
+        copy_z(z, z).wait_recv()
+    for z in range(n_gz):
+        firsts, seconds = entering_y(0, z)
+        for s, (part, line) in enumerate(zip(parts, lines_y)):
+            sums = [[jnp.zeros((rows, LANES), jnp.float32)] * 2 for _ in range(2)]
             for k in range(members):
-                summed = summed + anomalies[c, k, :, part].astype(jnp.float32) * field[k]
-            slots_z[gz, c, :, part] = summed
-
-    def copy_z(source, peer):
-        return pltpu.make_async_remote_copy(
-            src_ref=slots_z.at[source], dst_ref=slots_z.at[source],
-            send_sem=send_z.at[peer], recv_sem=recv_z.at[source],
-            device_id={"gz": peer}, device_id_type=MESH)
-
-    for off in range(1, n_gz):
-        copy_z(gz, lax.rem(gz + off, n_gz)).start()
-    for off in range(1, n_gz):
-        source = lax.rem(gz + off, n_gz)
-        copy_z(source, source).wait_recv()
-    grown = slots_z[0]
-    for t in range(1, n_gz):
-        grown = grown + slots_z[t]
-    grown = grown * spread
+                for e, state in enumerate((across(firsts[s], k), across(seconds[s], k))):
+                    for c in range(2):
+                        sums[c][e] = sums[c][e] + slots_a[z, c, k, :, part] * state
+            for c in range(2):
+                share = slots_z[z, c, :, part] + line.echo[0] * sums[c][0] + line.back[0] * sums[c][1]
+                increment[c, :, part] = share if z == 0 else increment[c, :, part] + share
+    grown = increment[...] * spread
     increment[...] = grown
     store_increment = pltpu.make_async_copy(increment, increment_h, store_sem.at[0])
     store_increment.start()
@@ -371,17 +355,19 @@
 
     leading = []
     for part, line in zip(parts, lines_y):
-        pulled = (anomalies[0, :, :, part].astype(jnp.float32) * back[None, :rows, part]
-                  + anomalies[1, :, :, part].astype(jnp.float32) * back[None, rows:, part])
+        pulled = (slots_a[gz, 0, :, :, part] * back[None, :rows, part]
+                  + slots_a[gz, 1, :, :, part] * back[None, rows:, part])
         leading.append(line.rates * pulled)
-    held = local_y(leading, lines_y, factors_y, 1)
+    outs = local_y(leading, lines_y, 1)
     start_y(1)
-    smoothed = finish_y(1, lines_y, factors_y, held)
+    each_y(1, lambda *source: copy_y(1, source, source).wait_recv())
+    firsts, seconds = entering_y(1, gz)
     leading = []
-    for part, line_x, line_y, field in zip(parts, lines_x, lines_y, smoothed):
+    for s, (part, line_x, line_y) in enumerate(zip(parts, lines_x, lines_y)):
         scale = (line_y.scales / line_y.rates * line_x.rates)[0]
+        echo, after = scale * line_y.echo[0], scale * line_y.back[0]
         for k in range(members):
-            work[k, :, part] = scale * field[k]
+            work[k, :, part] = scale * outs[s][k] + echo * across(firsts[s], k) + after * across(seconds[s], k)
         leading.append(work[:, :, part])
     held = local_x(leading, lines_x, 1, beyond)
     outgoing_x(1, lambda copy: copy.start())
@@ -416,23 +402,27 @@
     each_peer(lambda peer, place: copy_s(me, peer, place).wait_send())
     for turn in range(2):
         outgoing_x(turn, lambda copy: copy.wait_send())
-        for off in range(1, n_gy):
-            copy_y(turn, gy, lax.rem(gy + off, n_gy)).wait_send()
-    for off in range(1, n_gz):
-        copy_z(gz, lax.rem(gz + off, n_gz)).wait_send()
+        each_y(turn, lambda *peer: copy_y(turn, (gy, gz), peer).wait_send())
+    for z in other_z:
+        copy_z(gz, z).wait_send()
+        copy_a(gz, z).wait_send()
     store_increment.wait()
     store_gradient.wait()
     store_direction.wait()
 
 
 def results_kernel(*refs):
-    count = len(refs) // 2
+    count = len(refs) // 3
     sems = refs[-1]
-    copies = [pltpu.make_async_copy(refs[i], refs[count + i], sems.at[i]) for i in range(count)]
-    for copy in copies:
-        copy.start()
-    for copy in copies:
-        copy.wait()
+    loads = [pltpu.make_async_copy(refs[i], refs[2 * count + i], sems.at[0, i]) for i in range(count)]
+    stores = [pltpu.make_async_copy(refs[2 * count + i], refs[count + i], sems.at[1, i]) for i in range(count)]
+    for load in loads:
+        load.start()
+    for load, store in zip(loads, stores):
+        load.wait()
+        store.start()
+    for store in stores:
+        store.wait()
 
 
 def shards(
@@ -470,14 +460,15 @@
             pltpu.VMEM(controls.shape, jnp.float32),
             pltpu.VMEM((2, packed, columns), jnp.float32),
             pltpu.VMEM((2, n_gx, 2, packed, columns), jnp.float32),
-            pltpu.VMEM((2, n_gy, 2, rows, LANES), jnp.float32),
+            pltpu.VMEM((2, n_gy, n_gz, columns // LANES, 2, rows, LANES), jnp.float32),
             pltpu.VMEM((n_gz, 2, rows, columns), jnp.float32),
+            pltpu.VMEM((n_gz, *anomalies.shape), jnp.float32),
             pltpu.VMEM((total, 2, LANES), jnp.float32),
             pltpu.VMEM((columns, obs_cells.shape[-1])[::-1], jnp.bfloat16),
             dma((len(args),)), dma((3,)),
             dma((2, 2, n_gx)), dma((2, 2, n_gx)),
-            dma((2, n_gy)), dma((2, n_gy)),
-            dma((n_gz,)), dma((n_gz,)),
+            dma((2, n_gy, n_gz)), dma((2, n_gy, n_gz)),
+            dma((2, n_gz)), dma((2, n_gz)),
             dma((total,)), dma((total,)),
         ],
         compiler_params=pltpu.CompilerParams(
@@ -489,7 +480,7 @@
         out_shape=results,
         in_specs=[anywhere] * len(results),
         out_specs=(anywhere,) * len(results),
-        scratch_shapes=[dma((len(results),))],
+        scratch_shapes=[pltpu.VMEM(a.shape, a.dtype) for a in results] + [dma((2, len(results)))],
         compiler_params=pltpu.CompilerParams(vmem_limit_bytes=VMEM_BYTES),
     )(*held)
 

time: 41.3 us -> 31.3 us (0.76)
  Pallas kernels: 40.5 us -> 30.5 us
    pallas_call x1, Pallas kernels: 11.6 us -> 1.71 us  [shards(): pl.pallas_call(results_kernel, out_shape=results, in_specs=[anywhere] * l...]
where the time goes in v3:
time: 31.3 us; the launch traced here: 31.1 us
  Pallas kernels  30.5 us (97%)
  between operations  0.64 us (2%)
    pallas_call x1, Pallas kernels, shards(): pl.pallas_call(functools.partial(kernel, (n_gx, n_gy, n_gz)), out_shape=r...  28.8 us
    pallas_call x1, Pallas kernels, shards(): pl.pallas_call(results_kernel, out_shape=results, in_specs=[anywhere] * l...  1.71 us

profile of v3, /device:TPU:0, one launch (start us, length us, event | category | flops | bytes accessed | tf_op | source)
XLA Modules:
  0.0 31.1 jit_solution(16436452063745843701)
XLA Ops:
  0.6 28.8 %shard_map.121 = (f32[20,8,256]{2,1,0:T(8,128)}, f32[20,8,256]{2,1,0:T(8,128)}, f32[2,8,256]{2,1,0:T(8,128)}) custom-call(f32[20,8,256]{2,1,0:T(8,128)} %controls_h.1, bf16[2,20,8,256]{3,2,1,0:T(8,128)(2,1)} %anomalies_h.1, f32[8,256]{1,0:T(8,128)} %x_rates_h.1, f32[8,256]{1,0:T(8,128)} %y_rates_h.1, s32[1,1,512]{2,1,0:T(1,128)} %cells_h.1, ...), custom_call_target="tpu_custom_call" | custom-call | tf_op jit(solution)/shard_map/pallas_call | solution.py:451
  29.4 1.7 %shard_map.122 = (f32[20,8,256]{2,1,0:T(8,128)}, f32[20,8,256]{2,1,0:T(8,128)}, f32[2,8,256]{2,1,0:T(8,128)}) custom-call(f32[20,8,256]{2,1,0:T(8,128)} %get-tuple-element.6.refs_0_, f32[20,8,256]{2,1,0:T(8,128)} %get-tuple-element.7.refs_1_, f32[2,8,256]{2,1,0:T(8,128)} %get-tuple-element.8.refs_2_), custom_call_target="tpu_custom_call" | custom-call | tf_op jit(solution)/shard_map/pallas_call | solution.py:478

commit v4 on v3

--- a/solution.py
+++ b/solution.py
@@ -18,41 +18,57 @@
     return pltpu.roll(values, shift % values.shape[axis], axis)
 
 
-def ladder(rates, axis, reverse):
-    size = rates.shape[axis]
-    place = lax.broadcasted_iota(jnp.int32, rates.shape, axis)
-    factor = jnp.where(place == (size - 1 if reverse else 0), 0.0, rates)
-    steps = []
-    d = 1
-    while d < size:
-        shift = -d if reverse else d
-        steps.append((shift, factor))
-        factor = factor * rolled(factor, shift, axis)
-        d *= 2
-    return steps
-
-
-def run(steps, values, axis):
-    for shift, factor in steps:
-        values = values + factor * rolled(values, shift, axis)
-    return values
+def step_count(size):
+    return (size - 1).bit_length()
 
 
 class Line:
-    def __init__(self, rates, axis):
-        self.axis = axis
+    def __init__(self, rates, onward, back, echo):
         self.rates = rates
         self.scales = jnp.sqrt(1.0 - rates * rates)
-        self.forward = ladder(rates, axis, False)
-        self.backward = ladder(rates, axis, True)
-        place = lax.broadcasted_iota(jnp.int32, rates.shape, axis)
-        self.onward = run(self.forward, jnp.where(place == 0, rates, 0.0), axis)
-        self.back = run(self.backward, jnp.where(place == rates.shape[axis] - 1, rates, 0.0), axis)
-        self.echo = run(self.backward, self.scales * self.onward, axis)
+        self.onward, self.back, self.echo = onward, back, echo
+
+
+class Filter:
+    def __init__(self, rates, axis, ladder):
+        self.axis, self.ladder = axis, ladder
+        self.size = rates[0].shape[axis]
+        self.steps = step_count(self.size)
+        place = lax.broadcasted_iota(jnp.int32, rates[0].shape, axis)
+        first, last = place == 0, place == self.size - 1
+
+        def grow(step, factors):
+            grown = []
+            for at, factor in enumerate(factors):
+                way, group = divmod(at, len(rates))
+                ladder[way, group, step] = factor
+                grown.append(factor * pltpu.roll(factor, self.shift(step, way), axis))
+            return tuple(grown)
+
+        edges = [jnp.where(first, 0.0, r) for r in rates] + [jnp.where(last, 0.0, r) for r in rates]
+        lax.fori_loop(0, self.steps, grow, tuple(edges))
+        onward = self.run(0, [jnp.where(first, r, 0.0)[None] for r in rates])
+        back = self.run(1, [jnp.where(last, r, 0.0)[None] for r in rates])
+        scales = [jnp.sqrt(1.0 - r * r) for r in rates]
+        echo = self.run(1, [s * o for s, o in zip(scales, onward)])
+        self.lines = [Line(*each) for each in zip(rates, *([v[0] for v in vs] for vs in (onward, back, echo)))]
+
+    def shift(self, step, way):
+        reach = lax.shift_left(jnp.int32(1), jnp.int32(step))
+        return self.size - reach if way else reach
+
+    def run(self, way, values):
+        def advance(step, held):
+            shift = self.shift(step, way)
+            return tuple(
+                v + self.ladder[way, group, step][None] * pltpu.roll(v, shift, self.axis + 1)
+                for group, v in enumerate(held))
+
+        return lax.fori_loop(0, self.steps, advance, tuple(values))
 
     def local(self, leading):
-        inward = run(self.forward, leading, self.axis)
-        return inward, run(self.backward, self.scales * inward, self.axis)
+        inward = self.run(0, leading)
+        return inward, self.run(1, [line.scales * v for line, v in zip(self.lines, inward)])
 
 
 def split_three(values):
@@ -65,10 +81,10 @@
 
 def kernel(
     sizes,
-    controls_h, anomalies_h, x_rates_h, y_rates_h, cells_h, codes_h, values_h, weights_h, prev_h, old_h,
-    gradient_h, direction_h, increment_h,
-    controls, anomalies, x_rates, y_rates, cells, codes, values, weights, prev, old,
-    gradient, direction, increment, work, enter, slots_x, slots_y, slots_z, slots_a, slots_s, of_column,
+    controls_h, anomalies_h, x_rates_h, y_rates_h, cells_h, codes_h, values_h, weights_h, prev_h,
+    gradient_h, ratio_h, increment_h,
+    controls, anomalies, x_rates, y_rates, cells, codes, values, weights, prev,
+    gradient, ratio, increment, work, enter, slots_x, slots_y, slots_z, slots_a, slots_s, of_column, ladder_x, ladder_y,
     load_sem, store_sem, send_x, recv_x, send_y, recv_y, send_z, recv_z, send_s, recv_s,
 ):
     n_gx, n_gy, n_gz = sizes
@@ -102,7 +118,7 @@
         for i, (src, dst) in enumerate((
             (x_rates_h, x_rates), (controls_h, controls), (y_rates_h, y_rates),
             (anomalies_h, anomalies), (cells_h, cells), (codes_h, codes), (values_h, values),
-            (weights_h, weights), (prev_h, prev), (old_h, old)))
+            (weights_h, weights), (prev_h, prev)))
     ]
     for load in loads:
         load.start()
@@ -116,12 +132,12 @@
             tile = jnp.where(row_at == s, rolled(block, s - from_row, 0), tile)
         return tile
 
-    def local_x(leading, lines, turn, beyond=None):
+    def local_x(leading, turn, beyond=None):
         outs = []
-        for at, (part, line, lead) in enumerate(zip(parts, lines, leading)):
-            inward, outward = line.local(lead)
-            ends = [inward[k] for k in range(members)] + [line.onward[0]]
-            heads = [outward[k] for k in range(members)] + [line.echo[0]]
+        fields = along_x.local(leading)
+        for at, (part, line, inward, outward) in enumerate(zip(parts, along_x.lines, *fields)):
+            ends = [inward[k] for k in range(members)] + [line.onward]
+            heads = [outward[k] for k in range(members)] + [line.echo]
             for group in range(slots_x.shape[3] // rows):
                 here = pl.ds(group * rows, rows)
                 end = pack_rows(ends, rows - 1, group)
@@ -211,7 +227,7 @@
             for k in range(members):
                 first = jnp.broadcast_to(enter[0, k:k + 1, part], (rows, LANES))
                 second = jnp.broadcast_to(enter[1, k:k + 1, part], (rows, LANES))
-                work[k, :, part] = outward[k] + line.echo[0] * first + line.back[0] * second
+                work[k, :, part] = outward[k] + line.echo * first + line.back * second
             results.append(work[:, :, part])
         return results
 
@@ -224,14 +240,14 @@
     def across(tile, lane):
         return jnp.broadcast_to(tile[:, lane:lane + 1], (rows, LANES))
 
-    def local_y(leading, lines, turn):
+    def local_y(leading, turn):
         outs = []
-        for s, (line, lead) in enumerate(zip(lines, leading)):
-            inward, outward = line.local(lead)
+        fields = along_y.local(leading)
+        for s, (line, inward, outward) in enumerate(zip(along_y.lines, *fields)):
             slots_y[turn, gy, gz, s, 0] = jnp.where(
-                lane_at == members, across(line.onward[0], LANES - 1), pack_lanes(inward, LANES - 1))
+                lane_at == members, across(line.onward, LANES - 1), pack_lanes(inward, LANES - 1))
             slots_y[turn, gy, gz, s, 1] = jnp.where(
-                lane_at == members, across(line.echo[0], 0), pack_lanes(outward, 0))
+                lane_at == members, across(line.echo, 0), pack_lanes(outward, 0))
             outs.append(outward)
         return outs
 
@@ -282,14 +298,16 @@
     other_z = [lax.rem(gz + off, n_gz) for off in range(1, n_gz)]
 
     loads[0].wait()
-    lines_x = [Line(x_rates[:, part][None], 1) for part in parts]
+    along_x = Filter([x_rates[:, part] for part in parts], 0, ladder_x)
+    lines_x = along_x.lines
     loads[1].wait()
-    held = local_x([line.scales * controls[:, :, part] for part, line in zip(parts, lines_x)], lines_x, 0)
+    held = local_x([line.scales * controls[:, :, part] for part, line in zip(parts, lines_x)], 0)
     pl.semaphore_wait(barrier, total - 1)
     outgoing_x(0, lambda copy: copy.start())
 
     loads[2].wait()
-    lines_y = [Line(y_rates[:, part][None], 2) for part in parts]
+    along_y = Filter([y_rates[:, part] for part in parts], 1, ladder_y)
+    lines_y = along_y.lines
     for load in loads[3:]:
         load.wait()
     slots_a[gz] = anomalies[...].astype(jnp.float32)
@@ -313,7 +331,7 @@
 
     filtered = finish_x(0, lines_x, held)
 
-    outs = local_y([line.scales * v for line, v in zip(lines_y, filtered)], lines_y, 0)
+    outs = local_y([line.scales * v for line, v in zip(lines_y, filtered)], 0)
     start_y(0)
     for c in range(2):
         for part, field in zip(parts, outs):
@@ -321,7 +339,7 @@
     for z in other_z:
         copy_z(gz, z).start()
     responses = [response_x(part) for part in parts]
-    beyond = [line.onward[0, rows - 1:] * response for line, response in zip(lines_x, responses)]
+    beyond = [line.onward[rows - 1:] * response for line, response in zip(lines_x, responses)]
     for z in other_z:
         copy_a(z, z).wait_recv()
     each_y(0, lambda *source: copy_y(0, source, source).wait_recv())
@@ -336,7 +354,7 @@
                     for c in range(2):
                         sums[c][e] = sums[c][e] + slots_a[z, c, k, :, part] * state
             for c in range(2):
-                share = slots_z[z, c, :, part] + line.echo[0] * sums[c][0] + line.back[0] * sums[c][1]
+                share = slots_z[z, c, :, part] + line.echo * sums[c][0] + line.back * sums[c][1]
                 increment[c, :, part] = share if z == 0 else increment[c, :, part] + share
     grown = increment[...] * spread
     increment[...] = grown
@@ -358,18 +376,18 @@
         pulled = (slots_a[gz, 0, :, :, part] * back[None, :rows, part]
                   + slots_a[gz, 1, :, :, part] * back[None, rows:, part])
         leading.append(line.rates * pulled)
-    outs = local_y(leading, lines_y, 1)
+    outs = local_y(leading, 1)
     start_y(1)
     each_y(1, lambda *source: copy_y(1, source, source).wait_recv())
     firsts, seconds = entering_y(1, gz)
     leading = []
     for s, (part, line_x, line_y) in enumerate(zip(parts, lines_x, lines_y)):
-        scale = (line_y.scales / line_y.rates * line_x.rates)[0]
-        echo, after = scale * line_y.echo[0], scale * line_y.back[0]
+        scale = line_y.scales / line_y.rates * line_x.rates
+        echo, after = scale * line_y.echo, scale * line_y.back
         for k in range(members):
             work[k, :, part] = scale * outs[s][k] + echo * across(firsts[s], k) + after * across(seconds[s], k)
         leading.append(work[:, :, part])
-    held = local_x(leading, lines_x, 1, beyond)
+    held = local_x(leading, 1, beyond)
     outgoing_x(1, lambda copy: copy.start())
     smoothed = finish_x(1, lines_x, held, responses)
     numerator = jnp.zeros((rows, LANES), jnp.float32)
@@ -395,9 +413,9 @@
     each_peer(lambda peer, place: copy_s(me, peer, place).start())
     each_peer(lambda peer, place: copy_s(peer, peer, place).wait_recv())
     sums = jnp.sum(jnp.sum(slots_s[...], axis=0), axis=1, keepdims=True)
-    direction[...] = (sums[0:1] / sums[1:2])[None] * old[...] - gradient[...]
-    store_direction = pltpu.make_async_copy(direction, direction_h, store_sem.at[2])
-    store_direction.start()
+    ratio[...] = jnp.broadcast_to(sums[0:1] / sums[1:2], ratio.shape)
+    store_ratio = pltpu.make_async_copy(ratio, ratio_h, store_sem.at[2])
+    store_ratio.start()
 
     each_peer(lambda peer, place: copy_s(me, peer, place).wait_send())
     for turn in range(2):
@@ -408,19 +426,35 @@
         copy_a(gz, z).wait_send()
     store_increment.wait()
     store_gradient.wait()
-    store_direction.wait()
-
-
-def results_kernel(*refs):
-    count = len(refs) // 3
-    sems = refs[-1]
-    loads = [pltpu.make_async_copy(refs[i], refs[2 * count + i], sems.at[0, i]) for i in range(count)]
-    stores = [pltpu.make_async_copy(refs[2 * count + i], refs[count + i], sems.at[1, i]) for i in range(count)]
+    store_ratio.wait()
+
+
+def results_kernel(
+    gradient_h, ratio_h, increment_h, old_h, gradient_out, direction_out, increment_out,
+    gradient, ratio, increment, old, direction, load_sem, store_sem,
+):
+    loads = [
+        pltpu.make_async_copy(src, dst, load_sem.at[i])
+        for i, (src, dst) in enumerate((
+            (ratio_h, ratio), (gradient_h, gradient), (old_h, old), (increment_h, increment)))
+    ]
+    stores = [
+        pltpu.make_async_copy(src, dst, store_sem.at[i])
+        for i, (src, dst) in enumerate((
+            (gradient, gradient_out), (direction, direction_out), (increment, increment_out)))
+    ]
     for load in loads:
         load.start()
-    for load, store in zip(loads, stores):
-        load.wait()
-        store.start()
+    loads[0].wait()
+    loads[1].wait()
+    stores[0].start()
+    loads[2].wait()
+    for at in range(0, gradient.shape[2], LANES):
+        part = slice(at, at + LANES)
+        direction[:, :, part] = ratio[...][None] * old[:, :, part] - gradient[:, :, part]
+    stores[1].start()
+    loads[3].wait()
+    stores[2].start()
     for store in stores:
         store.wait()
 
@@ -441,13 +475,12 @@
     total = n_gx * n_gy * n_gz
     members, rows, columns = controls.shape
     packed = -(-(members + 1) // rows) * rows
-    args = (controls, anomalies, x_rates, y_rates, obs_cells, obs_codes, obs_values, obs_weights, prev_gradient,
-            prev_direction)
+    args = (controls, anomalies, x_rates, y_rates, obs_cells, obs_codes, obs_values, obs_weights, prev_gradient)
     dma = pltpu.SemaphoreType.DMA
     anywhere = pl.BlockSpec(memory_space=pl.ANY)
     results = tuple(
         jax.ShapeDtypeStruct(shape, jnp.float32)
-        for shape in (controls.shape, controls.shape, (2, rows, columns)))
+        for shape in (controls.shape, (rows, LANES), (2, rows, columns)))
     held = pl.pallas_call(
         functools.partial(kernel, (n_gx, n_gy, n_gz)),
         out_shape=results,
@@ -455,7 +488,7 @@
         out_specs=(anywhere,) * len(results),
         scratch_shapes=[pltpu.VMEM(a.shape, a.dtype) for a in args] + [
             pltpu.VMEM(controls.shape, jnp.float32),
-            pltpu.VMEM(controls.shape, jnp.float32),
+            pltpu.VMEM((rows, LANES), jnp.float32),
             pltpu.VMEM((2, rows, columns), jnp.float32),
             pltpu.VMEM(controls.shape, jnp.float32),
             pltpu.VMEM((2, packed, columns), jnp.float32),
@@ -464,7 +497,9 @@
             pltpu.VMEM((n_gz, 2, rows, columns), jnp.float32),
             pltpu.VMEM((n_gz, *anomalies.shape), jnp.float32),
             pltpu.VMEM((total, 2, LANES), jnp.float32),
-            pltpu.VMEM((columns, obs_cells.shape[-1])[::-1], jnp.bfloat16),
+            pltpu.VMEM((obs_cells.shape[-1], columns), jnp.bfloat16),
+            pltpu.VMEM((2, columns // LANES, step_count(rows), rows, LANES), jnp.float32),
+            pltpu.VMEM((2, columns // LANES, step_count(LANES), rows, LANES), jnp.float32),
             dma((len(args),)), dma((3,)),
             dma((2, 2, n_gx)), dma((2, 2, n_gx)),
             dma((2, n_gy, n_gz)), dma((2, n_gy, n_gz)),
@@ -475,12 +510,14 @@
             collective_id=0, has_side_effects=True, vmem_limit_bytes=VMEM_BYTES
         ),
     )(*args)
+    held = (*held, prev_direction)
+    outs = (held[0], prev_direction, held[2])
     return pl.pallas_call(
         results_kernel,
-        out_shape=results,
-        in_specs=[anywhere] * len(results),
-        out_specs=(anywhere,) * len(results),
-        scratch_shapes=[pltpu.VMEM(a.shape, a.dtype) for a in results] + [dma((2, len(results)))],
+        out_shape=tuple(jax.ShapeDtypeStruct(a.shape, a.dtype) for a in outs),
+        in_specs=[anywhere] * len(held),
+        out_specs=(anywhere,) * len(outs),
+        scratch_shapes=[pltpu.VMEM(a.shape, a.dtype) for a in (*held, prev_direction)] + [dma((4,)), dma((3,))],
         compiler_params=pltpu.CompilerParams(vmem_limit_bytes=VMEM_BYTES),
     )(*held)
 

time: 31.3 us -> 32.6 us (1.042)
  Pallas kernels: 30.5 us -> 31.7 us
    pallas_call x1, Pallas kernels: 28.8 us -> 29.9 us  [shards(): pl.pallas_call(functools.partial(kernel, (n_gx, n_gy, n_gz)), out_shape=r...]
where the time goes in v4:
time: 32.6 us; the launch traced here: 32.3 us
  Pallas kernels  31.7 us (97%)
  between operations  0.64 us (2%)
    pallas_call x1, Pallas kernels, shards(): pl.pallas_call(functools.partial(kernel, (n_gx, n_gy, n_gz)), out_shape=r...  29.9 us
    pallas_call x1, Pallas kernels, shards(): pl.pallas_call(results_kernel, out_shape=tuple((jax.ShapeDtypeStruct(a.sh...  1.75 us

profile of v4, /device:TPU:0, one launch (start us, length us, event | category | flops | bytes accessed | tf_op | source)
XLA Modules:
  0.0 32.3 jit_solution(7923561866369423776)
XLA Ops:
  0.6 29.9 %shard_map.121 = (f32[20,8,256]{2,1,0:T(8,128)}, f32[8,128]{1,0:T(8,128)}, f32[2,8,256]{2,1,0:T(8,128)}) custom-call(f32[20,8,256]{2,1,0:T(8,128)} %controls_h.1, bf16[2,20,8,256]{3,2,1,0:T(8,128)(2,1)} %anomalies_h.1, f32[8,256]{1,0:T(8,128)} %x_rates_h.1, f32[8,256]{1,0:T(8,128)} %y_rates_h.1, s32[1,1,512]{2,1,0:T(1,128)} %cells_h.1, ...), custom_call_target="tpu_custom_call" | custom-call | tf_op jit(solution)/shard_map/pallas_call | solution.py:484
  30.6 1.7 %shard_map.122 = (f32[20,8,256]{2,1,0:T(8,128)}, f32[20,8,256]{2,1,0:T(8,128)}, f32[2,8,256]{2,1,0:T(8,128)}) custom-call(f32[20,8,256]{2,1,0:T(8,128)} %get-tuple-element.6.gradient_h, f32[8,128]{1,0:T(8,128)} %get-tuple-element.7.ratio_h, f32[2,8,256]{2,1,0:T(8,128)} %get-tuple-element.8.increment_h, f32[20,8,256]{2,1,0:T(8,128)} %old_h.1), custom_call_target="tpu_custom_call" | custom-call | tf_op jit(solution)/shard_map/pallas_call | solution.py:515

commit v5 on v4

--- a/solution.py
+++ b/solution.py
@@ -37,38 +37,31 @@
         place = lax.broadcasted_iota(jnp.int32, rates[0].shape, axis)
         first, last = place == 0, place == self.size - 1
 
-        def grow(step, factors):
-            grown = []
-            for at, factor in enumerate(factors):
-                way, group = divmod(at, len(rates))
+        edges = [jnp.where(first, 0.0, r) for r in rates] + [jnp.where(last, 0.0, r) for r in rates]
+        for at, factor in enumerate(edges):
+            way, group = divmod(at, len(rates))
+            for step in range(self.steps):
                 ladder[way, group, step] = factor
-                grown.append(factor * pltpu.roll(factor, self.shift(step, way), axis))
-            return tuple(grown)
-
-        edges = [jnp.where(first, 0.0, r) for r in rates] + [jnp.where(last, 0.0, r) for r in rates]
-        lax.fori_loop(0, self.steps, grow, tuple(edges))
-        onward = self.run(0, [jnp.where(first, r, 0.0)[None] for r in rates])
-        back = self.run(1, [jnp.where(last, r, 0.0)[None] for r in rates])
-        scales = [jnp.sqrt(1.0 - r * r) for r in rates]
-        echo = self.run(1, [s * o for s, o in zip(scales, onward)])
-        self.lines = [Line(*each) for each in zip(rates, *([v[0] for v in vs] for vs in (onward, back, echo)))]
+                factor = factor * pltpu.roll(factor, self.shift(step, way), axis)
+        self.lines = []
+        for group, r in enumerate(rates):
+            onward = self.run(0, group, jnp.where(first, r, 0.0)[None])
+            back = self.run(1, group, jnp.where(last, r, 0.0)[None])
+            echo = self.run(1, group, jnp.sqrt(1.0 - r * r) * onward)
+            self.lines.append(Line(r, onward[0], back[0], echo[0]))
 
     def shift(self, step, way):
-        reach = lax.shift_left(jnp.int32(1), jnp.int32(step))
-        return self.size - reach if way else reach
-
-    def run(self, way, values):
-        def advance(step, held):
-            shift = self.shift(step, way)
-            return tuple(
-                v + self.ladder[way, group, step][None] * pltpu.roll(v, shift, self.axis + 1)
-                for group, v in enumerate(held))
-
-        return lax.fori_loop(0, self.steps, advance, tuple(values))
-
-    def local(self, leading):
-        inward = self.run(0, leading)
-        return inward, self.run(1, [line.scales * v for line, v in zip(self.lines, inward)])
+        return self.size - 2**step if way else 2**step
+
+    def run(self, way, group, values):
+        for step in range(self.steps):
+            values = values + self.ladder[way, group, step][None] * pltpu.roll(
+                values, self.shift(step, way), self.axis + 1)
+        return values
+
+    def local(self, group, leading):
+        inward = self.run(0, group, leading)
+        return inward, self.run(1, group, self.lines[group].scales * inward)
 
 
 def split_three(values):
@@ -132,104 +125,100 @@
             tile = jnp.where(row_at == s, rolled(block, s - from_row, 0), tile)
         return tile
 
-    def local_x(leading, turn, beyond=None):
-        outs = []
-        fields = along_x.local(leading)
-        for at, (part, line, inward, outward) in enumerate(zip(parts, along_x.lines, *fields)):
-            ends = [inward[k] for k in range(members)] + [line.onward]
-            heads = [outward[k] for k in range(members)] + [line.echo]
-            for group in range(slots_x.shape[3] // rows):
-                here = pl.ds(group * rows, rows)
-                end = pack_rows(ends, rows - 1, group)
-                head = pack_rows(heads, 0, group)
-                if beyond is not None:
-                    head = head + beyond[at] * end
-                slots_x[turn, gx, 0, here, part] = end
-                slots_x[turn, gx, 1, here, part] = head
-            outs.append(outward)
-        return outs
-
-    def copy_x(turn, kind, source, peer):
+    def local_x(at, leading, turn, beyond=None):
+        line = along_x.lines[at]
+        inward, outward = along_x.local(at, leading)
+        ends = [inward[k] for k in range(members)] + [line.onward]
+        heads = [outward[k] for k in range(members)] + [line.echo]
+        for group in range(slots_x.shape[4] // rows):
+            here = pl.ds(group * rows, rows)
+            end = pack_rows(ends, rows - 1, group)
+            head = pack_rows(heads, 0, group)
+            if beyond is not None:
+                head = head + beyond[at] * end
+            slots_x[turn, gx, 0, at, here] = end
+            slots_x[turn, gx, 1, at, here] = head
+        return outward
+
+    def copy_x(turn, kind, at, source, peer):
         return pltpu.make_async_remote_copy(
-            src_ref=slots_x.at[turn, source, kind], dst_ref=slots_x.at[turn, source, kind],
-            send_sem=send_x.at[turn, kind, peer], recv_sem=recv_x.at[turn, kind, source],
+            src_ref=slots_x.at[turn, source, kind, at], dst_ref=slots_x.at[turn, source, kind, at],
+            send_sem=send_x.at[turn, kind, at, peer], recv_sem=recv_x.at[turn, kind, at, source],
             device_id={"gx": peer}, device_id_type=MESH)
 
-    def outgoing_x(turn, act):
+    def outgoing_x(turn, at, act):
         for off in range(1, n_gx):
             peer = lax.rem(gx + off, n_gx)
 
             @pl.when(gx < n_gx - 1 if turn == 0 else peer > gx)
             def _():
-                act(copy_x(turn, 0, gx, peer))
+                act(copy_x(turn, 0, at, gx, peer))
 
             @pl.when(peer < gx)
             def _():
-                act(copy_x(turn, 1, gx, peer))
-
-    def incoming_x(turn):
+                act(copy_x(turn, 1, at, gx, peer))
+
+    def incoming_x(turn, at):
         for off in range(1, n_gx):
             source = lax.rem(gx + off, n_gx)
 
             @pl.when(source < n_gx - 1 if turn == 0 else source < gx)
             def _():
-                copy_x(turn, 0, source, source).wait_recv()
+                copy_x(turn, 0, at, source, source).wait_recv()
 
             @pl.when(source > gx)
             def _():
-                copy_x(turn, 1, source, source).wait_recv()
-
-    def states_x(turn, part):
-        state = jnp.zeros((slots_x.shape[3], LANES), jnp.float32)
+                copy_x(turn, 1, at, source, source).wait_recv()
+
+    def states_x(turn, at):
+        state = jnp.zeros((slots_x.shape[4], LANES), jnp.float32)
         states = [state]
         mine = state
         for t in range(n_gx - 1):
-            through = slots_x[0, t, 0, members:members + 1, part]
-            state = through * state + slots_x[turn, t, 0, :, part]
+            through = slots_x[0, t, 0, at, members:members + 1]
+            state = through * state + slots_x[turn, t, 0, at]
             states.append(state)
             mine = jnp.where(gx == t + 1, state, mine)
         return states, mine
 
-    def backward_x(turn, part, states):
-        state = jnp.zeros((slots_x.shape[3], LANES), jnp.float32)
+    def backward_x(turn, at, states):
+        state = jnp.zeros((slots_x.shape[4], LANES), jnp.float32)
         mine = state
         for t in range(n_gx - 1, 0, -1):
             if t < n_gx - 1:
-                state = slots_x[0, t, 0, members:members + 1, part] * state
-            state = state + slots_x[turn, t, 1, :, part]
+                state = slots_x[0, t, 0, at, members:members + 1] * state
+            state = state + slots_x[turn, t, 1, at]
             if states is not None:
-                state = state + slots_x[0, t, 1, members:members + 1, part] * states[t]
+                state = state + slots_x[0, t, 1, at, members:members + 1] * states[t]
             mine = jnp.where(gx == t - 1, state, mine)
         return mine
 
-    def response_x(part):
+    def response_x(at):
         factor = jnp.zeros((1, LANES), jnp.float32)
         mine = factor
         for t in range(n_gx - 1, 0, -1):
             if t < n_gx - 1:
-                through = slots_x[0, t, 0, members:members + 1, part]
+                through = slots_x[0, t, 0, at, members:members + 1]
                 factor = through * through * factor
-            factor = factor + slots_x[0, t, 1, members:members + 1, part]
+            factor = factor + slots_x[0, t, 1, at, members:members + 1]
             mine = jnp.where(gx == t - 1, factor, mine)
         return mine
 
-    def finish_x(turn, lines, outs, responses=None):
-        incoming_x(turn)
-        results = []
-        for at, (part, line, outward) in enumerate(zip(parts, lines, outs)):
-            states, mine = states_x(turn, part)
-            enter[0, :, part] = mine
-            if responses is None:
-                enter[1, :, part] = backward_x(turn, part, states)
-            else:
-                leaving = slots_x[0, gx, 0, members:members + 1, part] * mine + slots_x[turn, gx, 0, :, part]
-                enter[1, :, part] = backward_x(turn, part, None) + responses[at] * leaving
-            for k in range(members):
-                first = jnp.broadcast_to(enter[0, k:k + 1, part], (rows, LANES))
-                second = jnp.broadcast_to(enter[1, k:k + 1, part], (rows, LANES))
-                work[k, :, part] = outward[k] + line.echo * first + line.back * second
-            results.append(work[:, :, part])
-        return results
+    def finish_x(turn, at, outward, responses=None):
+        incoming_x(turn, at)
+        part, line = parts[at], along_x.lines[at]
+        states, mine = states_x(turn, at)
+        enter[0, :, part] = mine
+        if responses is None:
+            enter[1, :, part] = backward_x(turn, at, states)
+        else:
+            leaving = slots_x[0, gx, 0, at, members:members + 1] * mine + slots_x[turn, gx, 0, at]
+            enter[1, :, part] = backward_x(turn, at, None) + responses[at] * leaving
+        for k in range(members):
+            first = jnp.broadcast_to(enter[0, k:k + 1, part], (rows, LANES))
+            second = jnp.broadcast_to(enter[1, k:k + 1, part], (rows, LANES))
+            work[k, :, part] = outward[k] + line.echo * first + line.back * second
+        return work[:, :, part]
 
     def pack_lanes(field, from_lane):
         tile = jnp.zeros((rows, LANES), jnp.float32)
@@ -240,16 +229,14 @@
     def across(tile, lane):
         return jnp.broadcast_to(tile[:, lane:lane + 1], (rows, LANES))
 
-    def local_y(leading, turn):
-        outs = []
-        fields = along_y.local(leading)
-        for s, (line, inward, outward) in enumerate(zip(along_y.lines, *fields)):
-            slots_y[turn, gy, gz, s, 0] = jnp.where(
-                lane_at == members, across(line.onward, LANES - 1), pack_lanes(inward, LANES - 1))
-            slots_y[turn, gy, gz, s, 1] = jnp.where(
-                lane_at == members, across(line.echo, 0), pack_lanes(outward, 0))
-            outs.append(outward)
-        return outs
+    def local_y(s, leading, turn):
+        line = along_y.lines[s]
+        inward, outward = along_y.local(s, leading)
+        slots_y[turn, gy, gz, s, 0] = jnp.where(
+            lane_at == members, across(line.onward, LANES - 1), pack_lanes(inward, LANES - 1))
+        slots_y[turn, gy, gz, s, 1] = jnp.where(
+            lane_at == members, across(line.echo, 0), pack_lanes(outward, 0))
+        return outward
 
     def each_y(turn, act):
         for y, z in near[1:] if turn == 0 else [near[b * n_gz] for b in range(1, n_gy)]:
@@ -301,9 +288,12 @@
     along_x = Filter([x_rates[:, part] for part in parts], 0, ladder_x)
     lines_x = along_x.lines
     loads[1].wait()
-    held = local_x([line.scales * controls[:, :, part] for part, line in zip(parts, lines_x)], 0)
-    pl.semaphore_wait(barrier, total - 1)
-    outgoing_x(0, lambda copy: copy.start())
+    outs_x = []
+    for at, (part, line) in enumerate(zip(parts, lines_x)):
+        outs_x.append(local_x(at, line.scales * controls[:, :, part], 0))
+        if at == 0:
+            pl.semaphore_wait(barrier, total - 1)
+        outgoing_x(0, at, lambda copy: copy.start())
 
     loads[2].wait()
     along_y = Filter([y_rates[:, part] for part in parts], 1, ladder_y)
@@ -329,16 +319,15 @@
     before = prev[...]
     denominator = jnp.sum(jnp.sum(before * before, axis=0), axis=0, keepdims=True)
 
-    filtered = finish_x(0, lines_x, held)
-
-    outs = local_y([line.scales * v for line, v in zip(lines_y, filtered)], 0)
+    outs = [
+        local_y(at, line.scales * finish_x(0, at, outs_x[at]), 0) for at, line in enumerate(lines_y)]
     start_y(0)
     for c in range(2):
         for part, field in zip(parts, outs):
             slots_z[gz, c, :, part] = jnp.sum(slots_a[gz, c, :, :, part] * field, axis=0)
     for z in other_z:
         copy_z(gz, z).start()
-    responses = [response_x(part) for part in parts]
+    responses = [response_x(at) for at in range(len(parts))]
     beyond = [line.onward[rows - 1:] * response for line, response in zip(lines_x, responses)]
     for z in other_z:
         copy_a(z, z).wait_recv()
@@ -371,27 +360,25 @@
         split_three(toward * misfit), of_column[...], preferred_element_type=jnp.float32)
     back = (back[:2 * rows] + (back[2 * rows:4 * rows] + back[4 * rows:])) * spread
 
-    leading = []
-    for part, line in zip(parts, lines_y):
+    outs = []
+    for s, (part, line) in enumerate(zip(parts, lines_y)):
         pulled = (slots_a[gz, 0, :, :, part] * back[None, :rows, part]
                   + slots_a[gz, 1, :, :, part] * back[None, rows:, part])
-        leading.append(line.rates * pulled)
-    outs = local_y(leading, 1)
+        outs.append(local_y(s, line.rates * pulled, 1))
     start_y(1)
     each_y(1, lambda *source: copy_y(1, source, source).wait_recv())
     firsts, seconds = entering_y(1, gz)
-    leading = []
+    outs_x = []
     for s, (part, line_x, line_y) in enumerate(zip(parts, lines_x, lines_y)):
         scale = line_y.scales / line_y.rates * line_x.rates
         echo, after = scale * line_y.echo, scale * line_y.back
         for k in range(members):
             work[k, :, part] = scale * outs[s][k] + echo * across(firsts[s], k) + after * across(seconds[s], k)
-        leading.append(work[:, :, part])
-    held = local_x(leading, 1, beyond)
-    outgoing_x(1, lambda copy: copy.start())
-    smoothed = finish_x(1, lines_x, held, responses)
+        outs_x.append(local_x(s, work[:, :, part], 1, beyond))
+        outgoing_x(1, s, lambda copy: copy.start())
     numerator = jnp.zeros((rows, LANES), jnp.float32)
-    for part, line, field in zip(parts, lines_x, smoothed):
+    for at, (part, line) in enumerate(zip(parts, lines_x)):
+        field = finish_x(1, at, outs_x[at], responses)
         new = controls[:, :, part] + line.scales / line.rates * field
         gradient[:, :, part] = new
         numerator = numerator + jnp.sum(new * (new - prev[:, :, part]), axis=0)
@@ -419,7 +406,8 @@
 
     each_peer(lambda peer, place: copy_s(me, peer, place).wait_send())
     for turn in range(2):
-        outgoing_x(turn, lambda copy: copy.wait_send())
+        for at in range(len(parts)):
+            outgoing_x(turn, at, lambda copy: copy.wait_send())
         each_y(turn, lambda *peer: copy_y(turn, (gy, gz), peer).wait_send())
     for z in other_z:
         copy_z(gz, z).wait_send()
@@ -492,7 +480,7 @@
             pltpu.VMEM((2, rows, columns), jnp.float32),
             pltpu.VMEM(controls.shape, jnp.float32),
             pltpu.VMEM((2, packed, columns), jnp.float32),
-            pltpu.VMEM((2, n_gx, 2, packed, columns), jnp.float32),
+            pltpu.VMEM((2, n_gx, 2, columns // LANES, packed, LANES), jnp.float32),
             pltpu.VMEM((2, n_gy, n_gz, columns // LANES, 2, rows, LANES), jnp.float32),
             pltpu.VMEM((n_gz, 2, rows, columns), jnp.float32),
             pltpu.VMEM((n_gz, *anomalies.shape), jnp.float32),
@@ -501,7 +489,7 @@
             pltpu.VMEM((2, columns // LANES, step_count(rows), rows, LANES), jnp.float32),
             pltpu.VMEM((2, columns // LANES, step_count(LANES), rows, LANES), jnp.float32),
             dma((len(args),)), dma((3,)),
-            dma((2, 2, n_gx)), dma((2, 2, n_gx)),
+            dma((2, 2, columns // LANES, n_gx)), dma((2, 2, columns // LANES, n_gx)),
             dma((2, n_gy, n_gz)), dma((2, n_gy, n_gz)),
             dma((2, n_gz)), dma((2, n_gz)),
             dma((total,)), dma((total,)),

time: 32.6 us -> 31.7 us (0.972)
  Pallas kernels: 31.7 us -> 30.8 us
    pallas_call x1, Pallas kernels: 29.9 us -> 29.1 us  [shards(): pl.pallas_call(functools.partial(kernel, (n_gx, n_gy, n_gz)), out_shape=r...]
where the time goes in v5:
time: 31.7 us; the launch traced here: 31.5 us
  Pallas kernels  30.8 us (97%)
  between operations  0.64 us (2%)
    pallas_call x1, Pallas kernels, shards(): pl.pallas_call(functools.partial(kernel, (n_gx, n_gy, n_gz)), out_shape=r...  29.1 us
    pallas_call x1, Pallas kernels, shards(): pl.pallas_call(results_kernel, out_shape=tuple((jax.ShapeDtypeStruct(a.sh...  1.75 us

profile of v5, /device:TPU:0, one launch (start us, length us, event | category | flops | bytes accessed | tf_op | source)
XLA Modules:
  0.0 31.5 jit_solution(16678717625428882764)
XLA Ops:
  0.6 29.1 %shard_map.121 = (f32[20,8,256]{2,1,0:T(8,128)}, f32[8,128]{1,0:T(8,128)}, f32[2,8,256]{2,1,0:T(8,128)}) custom-call(f32[20,8,256]{2,1,0:T(8,128)} %controls_h.1, bf16[2,20,8,256]{3,2,1,0:T(8,128)(2,1)} %anomalies_h.1, f32[8,256]{1,0:T(8,128)} %x_rates_h.1, f32[8,256]{1,0:T(8,128)} %y_rates_h.1, s32[1,1,512]{2,1,0:T(1,128)} %cells_h.1, ...), custom_call_target="tpu_custom_call" | custom-call | tf_op jit(solution)/shard_map/pallas_call | solution.py:472
  29.7 1.7 %shard_map.122 = (f32[20,8,256]{2,1,0:T(8,128)}, f32[20,8,256]{2,1,0:T(8,128)}, f32[2,8,256]{2,1,0:T(8,128)}) custom-call(f32[20,8,256]{2,1,0:T(8,128)} %get-tuple-element.6.gradient_h, f32[8,128]{1,0:T(8,128)} %get-tuple-element.7.ratio_h, f32[2,8,256]{2,1,0:T(8,128)} %get-tuple-element.8.increment_h, f32[20,8,256]{2,1,0:T(8,128)} %old_h.1), custom_call_target="tpu_custom_call" | custom-call | tf_op jit(solution)/shard_map/pallas_call | solution.py:503

commit v6 on v5

--- a/solution.py
+++ b/solution.py
@@ -140,35 +140,24 @@
             slots_x[turn, gx, 1, at, here] = head
         return outward
 
-    def copy_x(turn, kind, at, source, peer):
+    def copy_x(turn, source, peer, leftward):
+        slot = (turn, source) if leftward and turn == 0 else (turn, source, 1 if leftward else 0)
         return pltpu.make_async_remote_copy(
-            src_ref=slots_x.at[turn, source, kind, at], dst_ref=slots_x.at[turn, source, kind, at],
-            send_sem=send_x.at[turn, kind, at, peer], recv_sem=recv_x.at[turn, kind, at, source],
+            src_ref=slots_x.at[slot], dst_ref=slots_x.at[slot],
+            send_sem=send_x.at[turn, peer], recv_sem=recv_x.at[turn, source],
             device_id={"gx": peer}, device_id_type=MESH)
 
-    def outgoing_x(turn, at, act):
+    def outgoing_x(turn, act):
         for off in range(1, n_gx):
             peer = lax.rem(gx + off, n_gx)
-
-            @pl.when(gx < n_gx - 1 if turn == 0 else peer > gx)
-            def _():
-                act(copy_x(turn, 0, at, gx, peer))
-
-            @pl.when(peer < gx)
-            def _():
-                act(copy_x(turn, 1, at, gx, peer))
-
-    def incoming_x(turn, at):
+            pl.when(peer > gx)(lambda: act(copy_x(turn, gx, peer, False)))
+            pl.when(peer < gx)(lambda: act(copy_x(turn, gx, peer, True)))
+
+    def incoming_x(turn):
         for off in range(1, n_gx):
             source = lax.rem(gx + off, n_gx)
-
-            @pl.when(source < n_gx - 1 if turn == 0 else source < gx)
-            def _():
-                copy_x(turn, 0, at, source, source).wait_recv()
-
-            @pl.when(source > gx)
-            def _():
-                copy_x(turn, 1, at, source, source).wait_recv()
+            pl.when(source < gx)(lambda: copy_x(turn, source, source, False).wait_recv())
+            pl.when(source > gx)(lambda: copy_x(turn, source, source, True).wait_recv())
 
     def states_x(turn, at):
         state = jnp.zeros((slots_x.shape[4], LANES), jnp.float32)
@@ -205,7 +194,6 @@
         return mine
 
     def finish_x(turn, at, outward, responses=None):
-        incoming_x(turn, at)
         part, line = parts[at], along_x.lines[at]
         states, mine = states_x(turn, at)
         enter[0, :, part] = mine
@@ -291,9 +279,8 @@
     outs_x = []
     for at, (part, line) in enumerate(zip(parts, lines_x)):
         outs_x.append(local_x(at, line.scales * controls[:, :, part], 0))
-        if at == 0:
-            pl.semaphore_wait(barrier, total - 1)
-        outgoing_x(0, at, lambda copy: copy.start())
+    pl.semaphore_wait(barrier, total - 1)
+    outgoing_x(0, lambda copy: copy.start())
 
     loads[2].wait()
     along_y = Filter([y_rates[:, part] for part in parts], 1, ladder_y)
@@ -319,6 +306,7 @@
     before = prev[...]
     denominator = jnp.sum(jnp.sum(before * before, axis=0), axis=0, keepdims=True)
 
+    incoming_x(0)
     outs = [
         local_y(at, line.scales * finish_x(0, at, outs_x[at]), 0) for at, line in enumerate(lines_y)]
     start_y(0)
@@ -375,7 +363,8 @@
         for k in range(members):
             work[k, :, part] = scale * outs[s][k] + echo * across(firsts[s], k) + after * across(seconds[s], k)
         outs_x.append(local_x(s, work[:, :, part], 1, beyond))
-        outgoing_x(1, s, lambda copy: copy.start())
+    outgoing_x(1, lambda copy: copy.start())
+    incoming_x(1)
     numerator = jnp.zeros((rows, LANES), jnp.float32)
     for at, (part, line) in enumerate(zip(parts, lines_x)):
         field = finish_x(1, at, outs_x[at], responses)
@@ -394,25 +383,28 @@
     def copy_s(source, peer, place):
         return pltpu.make_async_remote_copy(
             src_ref=slots_s.at[source], dst_ref=slots_s.at[source],
-            send_sem=send_s.at[peer], recv_sem=recv_s.at[source],
+            send_sem=send_s.at[0], recv_sem=recv_s.at[0],
             device_id=place, device_id_type=MESH)
 
     each_peer(lambda peer, place: copy_s(me, peer, place).start())
-    each_peer(lambda peer, place: copy_s(peer, peer, place).wait_recv())
-    sums = jnp.sum(jnp.sum(slots_s[...], axis=0), axis=1, keepdims=True)
-    ratio[...] = jnp.broadcast_to(sums[0:1] / sums[1:2], ratio.shape)
-    store_ratio = pltpu.make_async_copy(ratio, ratio_h, store_sem.at[2])
-    store_ratio.start()
-
-    each_peer(lambda peer, place: copy_s(me, peer, place).wait_send())
     for turn in range(2):
-        for at in range(len(parts)):
-            outgoing_x(turn, at, lambda copy: copy.wait_send())
+        outgoing_x(turn, lambda copy: copy.wait_send())
         each_y(turn, lambda *peer: copy_y(turn, (gy, gz), peer).wait_send())
     for z in other_z:
         copy_z(gz, z).wait_send()
         copy_a(gz, z).wait_send()
     store_increment.wait()
+    others = slots_s.at[pl.ds(0, total - 1)]
+    all_s = pltpu.make_async_remote_copy(
+        src_ref=others, dst_ref=others, send_sem=send_s.at[0], recv_sem=recv_s.at[0],
+        device_id={"gx": lax.rem(gx + 1, n_gx)}, device_id_type=MESH)
+    all_s.wait_recv()
+    sums = jnp.sum(jnp.sum(slots_s[...], axis=0), axis=1, keepdims=True)
+    ratio[...] = jnp.broadcast_to(sums[0:1] / sums[1:2], ratio.shape)
+    store_ratio = pltpu.make_async_copy(ratio, ratio_h, store_sem.at[2])
+    store_ratio.start()
+
+    all_s.wait_send()
     store_gradient.wait()
     store_ratio.wait()
 
@@ -489,10 +481,10 @@
             pltpu.VMEM((2, columns // LANES, step_count(rows), rows, LANES), jnp.float32),
             pltpu.VMEM((2, columns // LANES, step_count(LANES), rows, LANES), jnp.float32),
             dma((len(args),)), dma((3,)),
-            dma((2, 2, columns // LANES, n_gx)), dma((2, 2, columns // LANES, n_gx)),
+            dma((2, n_gx)), dma((2, n_gx)),
             dma((2, n_gy, n_gz)), dma((2, n_gy, n_gz)),
             dma((2, n_gz)), dma((2, n_gz)),
-            dma((total,)), dma((total,)),
+            dma((1,)), dma((1,)),
         ],
         compiler_params=pltpu.CompilerParams(
             collective_id=0, has_side_effects=True, vmem_limit_bytes=VMEM_BYTES

time: 31.7 us -> 31.9 us (level)
  no operation moved by 1% of the time
where the time goes in v6:
time: 31.9 us; the launch traced here: 31.7 us
  Pallas kernels  31.1 us (97%)
  between operations  0.64 us (2%)
    pallas_call x1, Pallas kernels, shards(): pl.pallas_call(functools.partial(kernel, (n_gx, n_gy, n_gz)), out_shape=r...  29.3 us
    pallas_call x1, Pallas kernels, shards(): pl.pallas_call(results_kernel, out_shape=tuple((jax.ShapeDtypeStruct(a.sh...  1.75 us

profile of v6, /device:TPU:0, one launch (start us, length us, event | category | flops | bytes accessed | tf_op | source)
XLA Modules:
  0.0 31.7 jit_solution(561034466923452509)
XLA Ops:
  0.6 29.3 %shard_map.121 = (f32[20,8,256]{2,1,0:T(8,128)}, f32[8,128]{1,0:T(8,128)}, f32[2,8,256]{2,1,0:T(8,128)}) custom-call(f32[20,8,256]{2,1,0:T(8,128)} %controls_h.1, bf16[2,20,8,256]{3,2,1,0:T(8,128)(2,1)} %anomalies_h.1, f32[8,256]{1,0:T(8,128)} %x_rates_h.1, f32[8,256]{1,0:T(8,128)} %y_rates_h.1, s32[1,1,512]{2,1,0:T(1,128)} %cells_h.1, ...), custom_call_target="tpu_custom_call" | custom-call | tf_op jit(solution)/shard_map/pallas_call | solution.py:464
  30.0 1.7 %shard_map.122 = (f32[20,8,256]{2,1,0:T(8,128)}, f32[20,8,256]{2,1,0:T(8,128)}, f32[2,8,256]{2,1,0:T(8,128)}) custom-call(f32[20,8,256]{2,1,0:T(8,128)} %get-tuple-element.6.gradient_h, f32[8,128]{1,0:T(8,128)} %get-tuple-element.7.ratio_h, f32[2,8,256]{2,1,0:T(8,128)} %get-tuple-element.8.increment_h, f32[20,8,256]{2,1,0:T(8,128)} %old_h.1), custom_call_target="tpu_custom_call" | custom-call | tf_op jit(solution)/shard_map/pallas_call | solution.py:495
